TPU v7x, 512 devices: a whole 4x4x16 slice. The times are simulated.
512 devices in a mesh: sec: 4 (over x), cell: 64 (over z, y), dir: 2 (over core).
Axes of the slice: x: 4, y: 4, z: 16, core: 2. Of those that a mesh axis runs over, the one named last changes fastest.
Arguments:
- volume_field: bfloat16 [49152, 256], P(('sec', 'cell')), may hold values from -6 to 6
- contrast_id: int32 [49152, 256], P(('sec', 'cell')), may hold values from 0 to 15
- contrast: float32 [16], replicated, may hold values from 0.1 to 2
- near_index: int32 [49152, 27], P(('sec', 'cell', 'dir')), may hold values from -1 to 287, as said below
- near_blocks: bfloat16 [27, 256, 256], replicated, may hold values from -0.078125 to 0.078125
- vol_radiation: bfloat16 [256, 256], P(None, 'dir'), may hold values from -0.375 to 0.375
- surf_radiation: bfloat16 [128, 256], P(None, 'dir'), may hold values from -0.5 to 0.5
- vol_receive: bfloat16 [256, 256], replicated, may hold values from -0.375 to 0.375
- surf_receive: bfloat16 [256, 128], replicated, may hold values from -0.375 to 0.375
- surface_current: bfloat16 [32768, 128], P(('sec', 'cell')), may hold values from -6 to 6
- surf_host: int32 [32768], P(('sec', 'cell')), may hold values from 0 to 191
- leaf_out: bfloat16 [192, 256], P(None, 'dir'), may hold values from -0.4375 to 0.4375
- leaf_in: bfloat16 [192, 256], P(None, 'dir'), may hold values from -4 to 4
- level_tables: float32 [4, 8, 256], P(None, None, 'dir'), may hold values from -4 to 4
- sv_blocks: bfloat16 [4, 128, 256], replicated, may hold values from -0.375 to 0.375
- pair_table: int32 [65536, 4, 3], P(('sec', 'cell', 'dir')), may hold values from -1 to 95, as said below
Outputs:
- volume_image: float32 [49152, 256], P(('sec', 'cell', 'dir'))
- surface_image: float32 [32768, 128], P(('sec', 'cell', 'dir'))
Inputs may be any that keep to these rules, and one draw needn't show every extreme that they name: `near_index`: entry w of row r names the leaf cell 192 * (r // 192) + w - 48, in a window that reaches 48 cells into each neighbouring coarse cell; -1 marks a missing block; the middle slot names the cell itself. `pair_table`: per slot: surface row among the core's 128 / 2 (-1 for an empty slot), volume row among the target core's 192 / 2, block kind. Live slots come first in each row; a row holds up to 4 pairs, and in every draw some target core receives 4 pairs from every core of its section.
All inputs are finite; a program needn't handle non-finite values.
Results may differ from a plain program's by a relative error of at most 0.0036.
Values may be sent and summed in bfloat16 or wider, within the bound.
A program may use at most 64 MiB of HBM per device.

v0:
```python
import jax
import jax.numpy as jnp
from jax import lax
from jax.sharding import PartitionSpec as P


def from_behind(x, axis, by):
    length = lax.axis_size(axis)
    pairs = [(i, i + by) for i in range(length) if 0 <= i + by < length]
    return lax.ppermute(x, axis, pairs)


def swapped(value, axis, distance):
    mask = 2**distance
    pairs = [(source, source ^ mask) for source in range(lax.axis_size(axis))]
    return lax.ppermute(value, axis, pairs)


def padded(cells, sides, width):
    for axis, dim in sides:
        count = lax.axis_size(axis)
        ends = count - 1
        head = lax.slice_in_dim(cells, 0, width, axis=dim)
        tail = lax.slice_in_dim(cells, cells.shape[dim] - width, cells.shape[dim], axis=dim)
        cells = jnp.concatenate(
            [
                lax.ppermute(tail, axis, [(i, (i + 1) % count) for i in range(ends)]),
                cells,
                lax.ppermute(head, axis, [((i + 1) % count, i) for i in range(ends)]),
            ],
            axis=dim,
        )
    return cells


def chain_tree(coarse_out, tables):
    levels = tables.shape[0]
    group_index = lax.axis_index(("sec", "cell"))
    current = coarse_out
    translated = []
    for level_id in range(levels):
        parity = group_index // 2**level_id % 2
        neighbours = []
        for offset in (-3, -2, 2, 3):
            neighbours.append(from_behind(current, ("sec", "cell"), -offset * 2**level_id))
        result = jnp.where(parity == 1, tables[level_id, 0] * neighbours[0], 0.0)
        result = result + tables[level_id, 1] * neighbours[1]
        result = result + tables[level_id, 2] * neighbours[2]
        result = result + jnp.where(parity == 0, tables[level_id, 3] * neighbours[3], 0.0)
        translated.append(result)
        if level_id + 1 < levels:
            partner = swapped(current, ("sec", "cell"), level_id)
            even_child = jnp.where(parity == 0, current, partner)
            odd_child = jnp.where(parity == 0, partner, current)
            current = tables[level_id, 4] * even_child + tables[level_id, 5] * odd_child
    downward = translated[-1]
    for level_id in range(levels - 2, -1, -1):
        parity = group_index // 2**level_id % 2
        shifted = jnp.where(parity == 1, tables[level_id, 7], tables[level_id, 6])
        downward = translated[level_id] + shifted * downward
    return downward


def on_device(
    volume_field,
    contrast_id,
    contrast,
    near_index,
    near_blocks,
    vol_radiation,
    surf_radiation,
    vol_receive,
    surf_receive,
    surface_current,
    surf_host,
    leaf_out,
    leaf_in,
    level_tables,
    sv_blocks,
    pair_table,
):
    dir_index = lax.axis_index("dir")
    leaf_count = volume_field.shape[0]
    half_rows = leaf_count // 2
    reach = leaf_count // 4
    half_surf = surface_current.shape[0] // 2
    width_vol = volume_field.shape[1]
    width_surf = surface_current.shape[1]
    contrast_map = jnp.zeros(volume_field.shape, jnp.float32)
    for material in range(contrast.shape[0]):
        contrast_map = contrast_map + jnp.where(contrast_id == material, contrast[material], 0.0)
    weighted = (volume_field.astype(jnp.float32) * contrast_map).astype(jnp.bfloat16)
    window = padded(weighted, ((("sec", "cell"), 0),), reach)
    padded_window = jnp.concatenate([window, jnp.zeros((1, width_vol), window.dtype)], axis=0)
    near_ids = jnp.where(near_index >= 0, near_index, window.shape[0])
    gathered = jnp.take(padded_window, near_ids.reshape(-1), axis=0).reshape(half_rows, -1)
    near_part = jnp.dot(
        gathered, near_blocks.reshape(-1, width_vol), preferred_element_type=jnp.float32
    )
    outgoing = jnp.dot(weighted, vol_radiation, preferred_element_type=jnp.float32)
    surf_waves = jnp.dot(surface_current, surf_radiation, preferred_element_type=jnp.float32)
    outgoing = outgoing + jax.ops.segment_sum(surf_waves, surf_host, num_segments=leaf_count)
    coarse_out = jnp.sum(leaf_out * outgoing, axis=0, keepdims=True)
    downward = chain_tree(coarse_out, level_tables)
    incoming = (leaf_in * downward).astype(jnp.bfloat16)
    wave_half = incoming.shape[1]
    recv_volume = lax.dynamic_slice_in_dim(vol_receive, dir_index * wave_half, wave_half, 0)
    recv_surface = lax.dynamic_slice_in_dim(surf_receive, dir_index * wave_half, wave_half, 0)
    far_volume = jnp.dot(incoming, recv_volume, preferred_element_type=jnp.float32)
    far_surface = jnp.dot(
        jnp.take(incoming, surf_host, axis=0), recv_surface, preferred_element_type=jnp.float32
    )
    far_volume, far_surface = (
        lax.psum_scatter(far_volume, "dir", scatter_dimension=0, tiled=True),
        lax.psum_scatter(far_surface, "dir", scatter_dimension=0, tiled=True),
    )
    own_current = lax.dynamic_slice_in_dim(surface_current, dir_index * half_surf, half_surf, 0)
    padded_current = jnp.concatenate(
        [own_current, jnp.zeros((1, width_surf), own_current.dtype)], axis=0
    )
    surf_slots = pair_table[:, :, 0]
    slot_ids = jnp.where(surf_slots >= 0, surf_slots, half_surf)
    sent_rows = jnp.take(padded_current, slot_ids.reshape(-1), axis=0).reshape(
        surf_slots.shape[0], surf_slots.shape[1], width_surf
    )
    slot_info = pair_table[:, :, 1:3]
    own_weighted = lax.dynamic_slice_in_dim(weighted, dir_index * half_rows, half_rows, 0)
    kinds_total = sv_blocks.shape[0]
    push_cat = jnp.transpose(sv_blocks, (1, 0, 2)).reshape(width_surf, -1)
    pull_cat = jnp.transpose(sv_blocks, (2, 0, 1)).reshape(width_vol, -1)
    arrived = lax.all_to_all(sent_rows, ("cell", "dir"), split_axis=0, concat_axis=0, tiled=True)
    arrived_info = lax.all_to_all(
        slot_info, ("cell", "dir"), split_axis=0, concat_axis=0, tiled=True
    )
    peer_count = arrived.shape[0]
    slot_count = arrived.shape[1]
    flat_rows = arrived.reshape(-1, width_surf)
    cell_ids = arrived_info[:, :, 0].reshape(-1)
    kind_mask = (
        arrived_info[:, :, 1].reshape(-1)[:, None]
        == jnp.arange(kinds_total, dtype=jnp.int32)[None, :]
    ).astype(jnp.float32)[:, :, None]
    pushed = jnp.dot(flat_rows, push_cat, preferred_element_type=jnp.float32).reshape(
        -1, kinds_total, width_vol
    )
    pushed = jnp.sum(pushed * kind_mask, axis=1)
    pulled_rows = jnp.take(own_weighted, cell_ids, axis=0)
    replies = jnp.dot(pulled_rows, pull_cat, preferred_element_type=jnp.float32).reshape(
        -1, kinds_total, width_surf
    )
    replies = jnp.sum(replies * kind_mask, axis=1).astype(jnp.bfloat16)
    returned = lax.all_to_all(
        replies.reshape(peer_count, slot_count, width_surf),
        ("cell", "dir"),
        split_axis=0,
        concat_axis=0,
        tiled=True,
    )
    returned, pushed, cell_ids = (
        returned,
        pushed.reshape(peer_count, slot_count, width_vol),
        cell_ids.reshape(peer_count, slot_count),
    )
    coupled_volume = jax.ops.segment_sum(
        pushed.reshape(-1, width_vol), cell_ids.reshape(-1), num_segments=half_rows
    )
    coupled_surface = jax.ops.segment_sum(
        returned.reshape(-1, width_surf).astype(jnp.float32),
        slot_ids.reshape(-1),
        num_segments=half_surf + 1,
    )[:half_surf]
    own_field = lax.dynamic_slice_in_dim(volume_field, dir_index * half_rows, half_rows, 0).astype(
        jnp.float32
    )
    volume_image = own_field + near_part + far_volume + coupled_volume
    surface_image = far_surface + coupled_surface
    return (volume_image, surface_image)


def solution(mesh):
    in_specs = (
        P(("sec", "cell"), None),
        P(("sec", "cell"), None),
        P(),
        P(("sec", "cell", "dir"), None),
        P(),
        P(None, "dir"),
        P(None, "dir"),
        P(),
        P(),
        P(("sec", "cell"), None),
        P(("sec", "cell")),
        P(None, "dir"),
        P(None, "dir"),
        P(None, None, "dir"),
        P(),
        P(("sec", "cell", "dir"), None, None),
    )
    out_specs = (P(("sec", "cell", "dir"), None), P(("sec", "cell", "dir"), None))
    return jax.shard_map(
        on_device, mesh=mesh, in_specs=in_specs, out_specs=out_specs, check_vma=False
    )
```

profile of v0, /device:TPU:1, one launch (start us, length us, event | category | flops | bytes accessed | tf_op | source)
XLA Modules:
  0.0 269.8 jit_solution(11500083093717406165)
XLA Ops:
  7.2 2.0 fusion.65
  9.2 11.6 %multiply_convert_fusion = bf16[192,256]{1,0:T(8,128)(2,1)S(1)} fusion(bf16[192,256]{1,0:T(8,128)(2,1)} %param.16, s32[192,256]{1,0:T(8,128)} %param.17, f32[]{:T(128)} %bitcast.15, f32[]{:T(128)} %bitcast.14, f32[]{:T(128)} %bitcast.13, f32[]{:T(128)} %bitcast.12, f32[]{:T(128)} %bitcast.11, f32[]{:T(128)} %bitcast.10, f32[]{:T(128)} %bitcast.9, ...), kind=kLoop, calls=%fused_computation.22 | loop fusion | flops 2457600 | bytes 393280 | tf_op jit(solution)/shard_map/convert_element_type | solution.py:92
  21.4 1.6 fusion.66
  23.0 1.5 fusion.67
  24.5 3.0 %scatter_fusion = f32[192,128]{1,0:T(8,128)} fusion(f32[192,128]{1,0:T(8,128)} %fusion.66, s32[128]{0:T(128)} %param.26, f32[128,128]{1,0:T(8,128)} %fusion.67), kind=kCustom, calls=%fused_computation.4 | custom fusion | flops 16384 | bytes 197120 | tf_op jit(solution)/shard_map/scatter-add | solution.py:102
  27.5 1.5 multiply_reduce_fusion.1
  29.0 4.0 %collective-permute-start.6 = (f32[1,128]{1,0:T(1,128)}, f32[1,128]{1,0:T(1,128)}, u32[]{:S(2)}, u32[]{:S(2)}) collective-permute-start(f32[1,128]{1,0:T(1,128)} %bitcast.18), channel_id=1, source_target_pairs={{0,2},{2,0},{4,6},{6,4},{8,10},{10,8},{12,14},{14,12},{16,18},{18,... | collective-permute-start | bytes 1544 | tf_op jit(solution)/shard_map/ppermute | solution.py:16
  33.0 4.3 %collective-permute-start.2 = (f32[1,128]{1,0:T(1,128)}, f32[1,128]{1,0:T(1,128)}, u32[]{:S(2)}, u32[]{:S(2)}) collective-permute-start(f32[1,128]{1,0:T(1,128)} %bitcast.18), channel_id=1, source_target_pairs={{0,6},{2,8},{4,10},{6,12},{8,14},{10,16},{12,18},{14,20},{16,22},{... | collective-permute-start | bytes 1544 | tf_op jit(solution)/shard_map/ppermute | solution.py:10
  37.4 3.8 %collective-permute-start.3 = (f32[1,128]{1,0:T(1,128)}, f32[1,128]{1,0:T(1,128)}, u32[]{:S(2)}, u32[]{:S(2)}) collective-permute-start(f32[1,128]{1,0:T(1,128)} %bitcast.18), channel_id=1, source_target_pairs={{0,4},{2,6},{4,8},{6,10},{8,12},{10,14},{12,16},{14,18},{16,20},{1... | collective-permute-start | bytes 1544 | tf_op jit(solution)/shard_map/ppermute | solution.py:10
  45.1 1.5 copy.32
  46.5 25.2 %all-to-all-start = ((s32[128,4,2]{1,2,0:T(2,128)}), s32[128,4,2]{1,2,0:T(2,128)}, u32[]{:S(2)}, u32[]{:S(2)}) async-start(s32[128,4,2]{1,2,0:T(2,128)} %copy.32), calls=%async_computation.1 | async-start | bytes 262144 | tf_op jit(solution)/shard_map/all_to_all | solution.py:132
  71.8 1.4 fusion.64
  77.5 1.4 copy.30
  82.7 4.8 %collective-permute-start.11 = (f32[1,128]{1,0:T(1,128)S(1)}, f32[1,128]{1,0:T(1,128)S(1)}, u32[]{:S(2)}, u32[]{:S(2)}) collective-permute-start(f32[1,128]{1,0:T(1,128)S(1)} %fusion.35), channel_id=1, source_target_pairs={{0,4},{2,6},{4,0},{6,2},{8,12},{10,14},{12,8},{14,10},{16,20},{18,... | collective-permute-start | bytes 1544 | tf_op jit(solution)/shard_map/ppermute | solution.py:16
  91.0 7.0 %collective-permute-start.7 = (f32[1,128]{1,0:T(1,128)S(1)}, f32[1,128]{1,0:T(1,128)}, u32[]{:S(2)}, u32[]{:S(2)}) collective-permute-start(f32[1,128]{1,0:T(1,128)S(1)} %fusion.35), channel_id=1, source_target_pairs={{0,12},{2,14},{4,16},{6,18},{8,20},{10,22},{12,24},{14,26},{16,28}... | collective-permute-start | bytes 1544 | tf_op jit(solution)/shard_map/ppermute | solution.py:10
  98.0 3.3 %collective-permute-start.16 = (f32[1,128]{1,0:T(1,128)S(1)}, f32[1,128]{1,0:T(1,128)}, u32[]{:S(2)}, u32[]{:S(2)}) collective-permute-start(f32[1,128]{1,0:T(1,128)S(1)} %fusion.44), channel_id=1, source_target_pairs={{0,8},{2,10},{4,12},{6,14},{8,0},{10,2},{12,4},{14,6},{16,24},{18,... | collective-permute-start | bytes 1544 | tf_op jit(solution)/shard_map/ppermute | solution.py:16
  101.3 2.0 collective-permute-start.8
  104.6 7.4 %collective-permute-start.12 = (f32[1,128]{1,0:T(1,128)S(1)}, f32[1,128]{1,0:T(1,128)S(1)}, u32[]{:S(2)}, u32[]{:S(2)}) collective-permute-start(f32[1,128]{1,0:T(1,128)S(1)} %fusion.44), channel_id=1, source_target_pairs={{0,24},{2,26},{4,28},{6,30},{8,32},{10,34},{12,36},{14,38},{16,40}... | collective-permute-start | bytes 1544 | tf_op jit(solution)/shard_map/ppermute | solution.py:10
  112.1 5.3 %collective-permute-start.13 = (f32[1,128]{1,0:T(1,128)S(1)}, f32[1,128]{1,0:T(1,128)S(1)}, u32[]{:S(2)}, u32[]{:S(2)}) collective-permute-start(f32[1,128]{1,0:T(1,128)S(1)} %fusion.44), channel_id=1, source_target_pairs={{0,16},{2,18},{4,20},{6,22},{8,24},{10,26},{12,28},{14,30},{16,32}... | collective-permute-start | bytes 1544 | tf_op jit(solution)/shard_map/ppermute | solution.py:10
  121.3 11.0 %collective-permute-start.17 = (f32[1,128]{1,0:T(1,128)}, f32[1,128]{1,0:T(1,128)S(1)}, u32[]{:S(2)}, u32[]{:S(2)}) collective-permute-start(f32[1,128]{1,0:T(1,128)} %fusion.53), channel_id=1, source_target_pairs={{0,48},{2,50},{4,52},{6,54},{8,56},{10,58},{12,60},{14,62},{16,64}... | collective-permute-start | bytes 1544 | tf_op jit(solution)/shard_map/ppermute | solution.py:10
  132.3 4.9 %collective-permute-start.18 = (f32[1,128]{1,0:T(1,128)}, f32[1,128]{1,0:T(1,128)}, u32[]{:S(2)}, u32[]{:S(2)}) collective-permute-start(f32[1,128]{1,0:T(1,128)} %fusion.53), channel_id=1, source_target_pairs={{0,32},{2,34},{4,36},{6,38},{8,40},{10,42},{12,44},{14,46},{16,48}... | collective-permute-start | bytes 1544 | tf_op jit(solution)/shard_map/ppermute | solution.py:10
  140.4 3.7 %collective-permute-start = (bf16[48,256]{1,0:T(8,128)(2,1)}, bf16[48,256]{1,0:T(8,128)(2,1)}, u32[]{:S(2)}, u32[]{:S(2)}) collective-permute-start(bf16[48,256]{1,0:T(8,128)(2,1)} %get-tuple-element.5), channel_id=1, source_target_pairs={{0,2},{2,4},{4,6},{6,8},{8,10},{10,12},{12,14},{14,16},{16,18},{18... | collective-permute-start | bytes 73736 | tf_op jit(solution)/shard_map/ppermute | solution.py:27
  145.6 5.4 %collective-permute-done.20 = f32[1,128]{1,0:T(1,128)} collective-permute-done((f32[1,128]{1,0:T(1,128)}, f32[1,128]{1,0:T(1,128)}, u32[]{:S(2)}, u32[]{:S(2)}) %collective-permute-start.20) | collective-permute-done | bytes 544 | tf_op jit(solution)/shard_map/ppermute | solution.py:10
  153.5 1.7 fusion.19
  156.6 1.4 copy.29
  158.7 1.5 squeeze.76
  160.9 1.8 copy.35
  164.7 1.4 constant_dynamic-slice_fusion
  166.1 2.2 gather_fusion.2
  168.3 1.6 fusion.21
  169.9 2.4 slice_reduce_fusion
  172.3 1.5 broadcast_in_dim_reshape_reshape_reshape_squeeze.3
  175.7 2.5 gather_fusion.1
  178.2 1.7 broadcast_select_fusion.1
  180.0 22.4 %all-to-all-start.1 = ((bf16[128,4,128]{2,1,0:T(4,128)(2,1)}), bf16[128,4,128]{2,1,0:T(4,128)(2,1)}, u32[]{:S(2)}, u32[]{:S(2)}) async-start(bf16[128,4,128]{2,1,0:T(4,128)(2,1)} %broadcast_select_fusion.1), calls=%async_computation.2 | async-start | bytes 262144 | tf_op jit(solution)/shard_map/all_to_all | solution.py:131
  206.2 3.1 %gather_fusion.3 = bf16[512,256]{1,0:T(8,128)(2,1)} fusion(bf16[96,256]{1,0:T(8,128)(2,1)} %constant_dynamic-slice_fusion, s32[1024]{0:T(1024)} %pad_clamp_fusion.1), kind=kCustom, calls=%fused_computation.3 | custom fusion | bytes 526336 | tf_op jit(solution)/shard_map/jit(_take)/gather | solution.py:147
  209.3 2.1 fusion.2
  211.5 1.7 maximum_maximum_fusion
  213.2 8.3 %gather_fusion = bf16[2592,256]{1,0:T(8,128)(2,1)} fusion(bf16[289,256]{1,0:T(8,128)(2,1)} %maximum_maximum_fusion, s32[3072]{0:T(1024)S(1)} %copy-done.5), kind=kCustom, calls=%fused_computation | custom fusion | bytes 2664576 | tf_op jit(solution)/shard_map/jit(_take)/gather | solution.py:96
  221.5 3.2 %gather.21 = bf16[96,27,256]{2,1,0:T(8,128)(2,1)} reshape(bf16[2592,256]{1,0:T(8,128)(2,1)} %gather_fusion) | data formatting | bytes 2654208 | tf_op jit(solution)/shard_map/jit(_take)/gather | solution.py:96
  224.7 16.6 %all-to-all-start.2 = ((bf16[128,4,128]{2,1,0:T(4,128)(2,1)}), bf16[128,4,128]{2,1,0:T(4,128)(2,1)}, u32[]{:S(2)}, u32[]{:S(2)}) async-start(bf16[128,4,128]{2,1,0:T(4,128)(2,1)} %bitcast.215), calls=%async_computation.4 | async-start | bytes 262144 | tf_op jit(solution)/shard_map/all_to_all | solution.py:152
  241.3 2.6 broadcast_select_fusion
  244.0 3.9 %fusion.9 = f32[96,256]{1,0:T(8,128)} fusion(f32[96,256]{1,0:T(8,128)} %reduce-scatter.3.cloned.1.call-done, bf16[27,256,256]{2,1,0:T(8,128)(2,1)S(1)} %copy-done, bf16[96,27,256]{2,1,0:T(8,128)(2,1)} %broadcast_select_fusion, bf16[192,256]{1,0:T(8,128)(2,1)} %param.16, s32[]{:T(128)S(6)} %select_n.323), kind=kOutput, calls=%fused_computation.15 | convolution fusion | flops 339812352 | bytes 5111812 | tf_op jit(solution)/shard_map/dot_general | solution.py:97
  247.8 2.2 multiply_reduce_fusion
  250.0 5.0 %scatter_fusion.1 = f32[96,256]{1,0:T(8,128)} fusion(f32[96,256]{1,0:T(8,128)} %fusion.9, s32[512]{0:T(512)S(1)} %reshape.285, f32[512,256]{1,0:T(8,128)} %multiply_reduce_fusion), kind=kCustom, calls=%fused_computation.5 | custom fusion | flops 131072 | bytes 1574912 | tf_op jit(solution)/shard_map/scatter-add | solution.py:164
  255.0 2.4 all-to-all-done.2
  257.5 4.1 %scatter_custom_fusion.2 = f32[65,128]{1,0:T(8,128)} fusion(s32[512]{0:T(512)} %bitcast.218, bf16[512,128]{1,0:T(8,128)(2,1)} %bitcast.69, f32[]{:T(128)} %constant.166.clone.1), kind=kCustom, calls=%fused_computation.16 | custom fusion | flops 131072 | bytes 164864 | tf_op jit(solution)/shard_map/scatter-add | solution.py:167
  261.5 1.4 slice_add_fusion
  (93 shorter events, 38.8 us)
Async XLA Ops:
  7.2 236.8 %copy-start = (bf16[27,256,256]{2,1,0:T(8,128)(2,1)S(1)}, bf16[27,256,256]{2,1,0:T(8,128)(2,1)}, u32[]{:S(2)}) copy-start(bf16[27,256,256]{2,1,0:T(8,128)(2,1)} %param.20) | copy-start | bytes 10616836
  7.2 66.0 %copy-start.4 = (s32[96,27]{0,1:T(8,128)S(1)}, s32[96,27]{0,1:T(8,128)}, u32[]{:S(2)}) copy-start(s32[96,27]{0,1:T(8,128)} %param.19) | copy-start | bytes 31108
  20.7 0.6 copy-start.2
  29.0 52.9 %collective-permute-start.6 = (f32[1,128]{1,0:T(1,128)}, f32[1,128]{1,0:T(1,128)}, u32[]{:S(2)}, u32[]{:S(2)}) collective-permute-start(f32[1,128]{1,0:T(1,128)} %bitcast.18), channel_id=1, source_target_pairs={{0,2},{2,0},{4,6},{6,4},{8,10},{10,8},{12,14},{14,12},{16,18},{18,... | collective-permute-start | bytes 1544 | tf_op jit(solution)/shard_map/ppermute | solution.py:16
  33.0 58.0 %collective-permute-start.2 = (f32[1,128]{1,0:T(1,128)}, f32[1,128]{1,0:T(1,128)}, u32[]{:S(2)}, u32[]{:S(2)}) collective-permute-start(f32[1,128]{1,0:T(1,128)} %bitcast.18), channel_id=1, source_target_pairs={{0,6},{2,8},{4,10},{6,12},{8,14},{10,16},{12,18},{14,20},{16,22},{... | collective-permute-start | bytes 1544 | tf_op jit(solution)/shard_map/ppermute | solution.py:10
  37.4 60.6 %collective-permute-start.3 = (f32[1,128]{1,0:T(1,128)}, f32[1,128]{1,0:T(1,128)}, u32[]{:S(2)}, u32[]{:S(2)}) collective-permute-start(f32[1,128]{1,0:T(1,128)} %bitcast.18), channel_id=1, source_target_pairs={{0,4},{2,6},{4,8},{6,10},{8,12},{10,14},{12,16},{14,18},{16,20},{1... | collective-permute-start | bytes 1544 | tf_op jit(solution)/shard_map/ppermute | solution.py:10
  41.2 60.1 %collective-permute-start.4 = (f32[1,128]{1,0:T(1,128)}, f32[1,128]{1,0:T(1,128)}, u32[]{:S(2)}, u32[]{:S(2)}) collective-permute-start(f32[1,128]{1,0:T(1,128)} %bitcast.18), channel_id=1, source_target_pairs={{4,0},{6,2},{8,4},{10,6},{12,8},{14,10},{16,12},{18,14},{20,16},{2... | collective-permute-start | bytes 1544 | tf_op jit(solution)/shard_map/ppermute | solution.py:10
  42.5 60.8 %collective-permute-start.5 = (f32[1,128]{1,0:T(1,128)}, f32[1,128]{1,0:T(1,128)}, u32[]{:S(2)}, u32[]{:S(2)}) collective-permute-start(f32[1,128]{1,0:T(1,128)} %bitcast.18), channel_id=1, source_target_pairs={{6,0},{8,2},{10,4},{12,6},{14,8},{16,10},{18,12},{20,14},{22,16},{... | collective-permute-start | bytes 1544 | tf_op jit(solution)/shard_map/ppermute | solution.py:10
  46.5 123.3 %all-to-all-start = ((s32[128,4,2]{1,2,0:T(2,128)}), s32[128,4,2]{1,2,0:T(2,128)}, u32[]{:S(2)}, u32[]{:S(2)}) async-start(s32[128,4,2]{1,2,0:T(2,128)} %copy.32), calls=%async_computation.1 | async-start | bytes 262144 | tf_op jit(solution)/shard_map/all_to_all | solution.py:132
  71.8 172.2 %reduce-scatter.3.cloned.1.call-start = ((), (), s32[]{:S(2)}) async-start(), calls=%async_computation.5 | async-start | bytes 294912 | tf_op jit(solution)/shard_map/reduce_scatter | solution.py:114
  82.7 5.8 %collective-permute-start.11 = (f32[1,128]{1,0:T(1,128)S(1)}, f32[1,128]{1,0:T(1,128)S(1)}, u32[]{:S(2)}, u32[]{:S(2)}) collective-permute-start(f32[1,128]{1,0:T(1,128)S(1)} %fusion.35), channel_id=1, source_target_pairs={{0,4},{2,6},{4,0},{6,2},{8,12},{10,14},{12,8},{14,10},{16,20},{18,... | collective-permute-start | bytes 1544 | tf_op jit(solution)/shard_map/ppermute | solution.py:16
  88.4 0.5 copy-start.13
  89.0 15.6 %collective-permute-start.10 = (f32[1,128]{1,0:T(1,128)S(1)}, f32[1,128]{1,0:T(1,128)S(1)}, u32[]{:S(2)}, u32[]{:S(2)}) collective-permute-start(f32[1,128]{1,0:T(1,128)S(1)} %fusion.35), channel_id=1, source_target_pairs={{12,0},{14,2},{16,4},{18,6},{20,8},{22,10},{24,12},{26,14},{28,16}... | collective-permute-start | bytes 1544 | tf_op jit(solution)/shard_map/ppermute | solution.py:10
  91.0 21.0 %collective-permute-start.7 = (f32[1,128]{1,0:T(1,128)S(1)}, f32[1,128]{1,0:T(1,128)}, u32[]{:S(2)}, u32[]{:S(2)}) collective-permute-start(f32[1,128]{1,0:T(1,128)S(1)} %fusion.35), channel_id=1, source_target_pairs={{0,12},{2,14},{4,16},{6,18},{8,20},{10,22},{12,24},{14,26},{16,28}... | collective-permute-start | bytes 1544 | tf_op jit(solution)/shard_map/ppermute | solution.py:10
  98.0 19.4 %collective-permute-start.16 = (f32[1,128]{1,0:T(1,128)S(1)}, f32[1,128]{1,0:T(1,128)}, u32[]{:S(2)}, u32[]{:S(2)}) collective-permute-start(f32[1,128]{1,0:T(1,128)S(1)} %fusion.44), channel_id=1, source_target_pairs={{0,8},{2,10},{4,12},{6,14},{8,0},{10,2},{12,4},{14,6},{16,24},{18,... | collective-permute-start | bytes 1544 | tf_op jit(solution)/shard_map/ppermute | solution.py:16
  101.3 18.7 %collective-permute-start.8 = (f32[1,128]{1,0:T(1,128)S(1)}, f32[1,128]{1,0:T(1,128)S(1)}, u32[]{:S(2)}, u32[]{:S(2)}) collective-permute-start(f32[1,128]{1,0:T(1,128)S(1)} %fusion.35), channel_id=1, source_target_pairs={{0,8},{2,10},{4,12},{6,14},{8,16},{10,18},{12,20},{14,22},{16,24},... | collective-permute-start | bytes 1544 | tf_op jit(solution)/shard_map/ppermute | solution.py:10
  103.3 18.0 %collective-permute-start.9 = (f32[1,128]{1,0:T(1,128)S(1)}, f32[1,128]{1,0:T(1,128)S(1)}, u32[]{:S(2)}, u32[]{:S(2)}) collective-permute-start(f32[1,128]{1,0:T(1,128)S(1)} %fusion.35), channel_id=1, source_target_pairs={{8,0},{10,2},{12,4},{14,6},{16,8},{18,10},{20,12},{22,14},{24,16},... | collective-permute-start | bytes 1544 | tf_op jit(solution)/shard_map/ppermute | solution.py:10
  104.6 27.7 %collective-permute-start.12 = (f32[1,128]{1,0:T(1,128)S(1)}, f32[1,128]{1,0:T(1,128)S(1)}, u32[]{:S(2)}, u32[]{:S(2)}) collective-permute-start(f32[1,128]{1,0:T(1,128)S(1)} %fusion.44), channel_id=1, source_target_pairs={{0,24},{2,26},{4,28},{6,30},{8,32},{10,34},{12,36},{14,38},{16,40}... | collective-permute-start | bytes 1544 | tf_op jit(solution)/shard_map/ppermute | solution.py:10
  112.1 25.1 %collective-permute-start.13 = (f32[1,128]{1,0:T(1,128)S(1)}, f32[1,128]{1,0:T(1,128)S(1)}, u32[]{:S(2)}, u32[]{:S(2)}) collective-permute-start(f32[1,128]{1,0:T(1,128)S(1)} %fusion.44), channel_id=1, source_target_pairs={{0,16},{2,18},{4,20},{6,22},{8,24},{10,26},{12,28},{14,30},{16,32}... | collective-permute-start | bytes 1544 | tf_op jit(solution)/shard_map/ppermute | solution.py:10
  117.4 21.1 %collective-permute-start.14 = (f32[1,128]{1,0:T(1,128)S(1)}, f32[1,128]{1,0:T(1,128)S(1)}, u32[]{:S(2)}, u32[]{:S(2)}) collective-permute-start(f32[1,128]{1,0:T(1,128)S(1)} %fusion.44), channel_id=1, source_target_pairs={{16,0},{18,2},{20,4},{22,6},{24,8},{26,10},{28,12},{30,14},{32,16}... | collective-permute-start | bytes 1544 | tf_op jit(solution)/shard_map/ppermute | solution.py:10
  120.0 18.5 %copy-start.8 = (f32[1,128]{1,0:T(1,128)}, f32[1,128]{1,0:T(1,128)S(1)}, u32[]{:S(2)}) copy-start(f32[1,128]{1,0:T(1,128)S(1)} %collective-permute-done.8) | copy-start | bytes 1540
  120.0 20.4 %collective-permute-start.15 = (f32[1,128]{1,0:T(1,128)S(1)}, f32[1,128]{1,0:T(1,128)}, u32[]{:S(2)}, u32[]{:S(2)}) collective-permute-start(f32[1,128]{1,0:T(1,128)S(1)} %fusion.44), channel_id=1, source_target_pairs={{24,0},{26,2},{28,4},{30,6},{32,8},{34,10},{36,12},{38,14},{40,16}... | collective-permute-start | bytes 1544 | tf_op jit(solution)/shard_map/ppermute | solution.py:10
  121.3 17.2 %copy-start.9 = (f32[1,128]{1,0:T(1,128)}, f32[1,128]{1,0:T(1,128)S(1)}, u32[]{:S(2)}) copy-start(f32[1,128]{1,0:T(1,128)S(1)} %collective-permute-done.9) | copy-start | bytes 1540
  121.3 22.8 %collective-permute-start.17 = (f32[1,128]{1,0:T(1,128)}, f32[1,128]{1,0:T(1,128)S(1)}, u32[]{:S(2)}, u32[]{:S(2)}) collective-permute-start(f32[1,128]{1,0:T(1,128)} %fusion.53), channel_id=1, source_target_pairs={{0,48},{2,50},{4,52},{6,54},{8,56},{10,58},{12,60},{14,62},{16,64}... | collective-permute-start | bytes 1544 | tf_op jit(solution)/shard_map/ppermute | solution.py:10
  132.3 6.2 %copy-start.10 = (f32[1,128]{1,0:T(1,128)}, f32[1,128]{1,0:T(1,128)S(1)}, u32[]{:S(2)}) copy-start(f32[1,128]{1,0:T(1,128)S(1)} %collective-permute-done.12) | copy-start | bytes 1540
  132.3 13.0 %collective-permute-start.18 = (f32[1,128]{1,0:T(1,128)}, f32[1,128]{1,0:T(1,128)}, u32[]{:S(2)}, u32[]{:S(2)}) collective-permute-start(f32[1,128]{1,0:T(1,128)} %fusion.53), channel_id=1, source_target_pairs={{0,32},{2,34},{4,36},{6,38},{8,40},{10,42},{12,44},{14,46},{16,48}... | collective-permute-start | bytes 1544 | tf_op jit(solution)/shard_map/ppermute | solution.py:10
  137.2 1.3 copy-start.11
  137.2 8.4 %collective-permute-start.19 = (f32[1,128]{1,0:T(1,128)}, f32[1,128]{1,0:T(1,128)}, u32[]{:S(2)}, u32[]{:S(2)}) collective-permute-start(f32[1,128]{1,0:T(1,128)} %fusion.53), channel_id=1, source_target_pairs={{32,0},{34,2},{36,4},{38,6},{40,8},{42,10},{44,12},{46,14},{48,16}... | collective-permute-start | bytes 1544 | tf_op jit(solution)/shard_map/ppermute | solution.py:10
  138.5 0.5 copy-start.12
  139.1 12.0 %collective-permute-start.20 = (f32[1,128]{1,0:T(1,128)}, f32[1,128]{1,0:T(1,128)}, u32[]{:S(2)}, u32[]{:S(2)}) collective-permute-start(f32[1,128]{1,0:T(1,128)} %fusion.53), channel_id=1, source_target_pairs={{48,0},{50,2},{52,4},{54,6},{56,8},{58,10},{60,12},{62,14},{64,16}... | collective-permute-start | bytes 1544 | tf_op jit(solution)/shard_map/ppermute | solution.py:10
  140.4 71.1 %collective-permute-start = (bf16[48,256]{1,0:T(8,128)(2,1)}, bf16[48,256]{1,0:T(8,128)(2,1)}, u32[]{:S(2)}, u32[]{:S(2)}) collective-permute-start(bf16[48,256]{1,0:T(8,128)(2,1)} %get-tuple-element.5), channel_id=1, source_target_pairs={{0,2},{2,4},{4,6},{6,8},{8,10},{10,12},{12,14},{14,16},{16,18},{18... | collective-permute-start | bytes 73736 | tf_op jit(solution)/shard_map/ppermute | solution.py:27
  144.1 67.4 %collective-permute-start.1 = (bf16[48,256]{1,0:T(8,128)(2,1)}, bf16[48,256]{1,0:T(8,128)(2,1)}, u32[]{:S(2)}, u32[]{:S(2)}) collective-permute-start(bf16[48,256]{1,0:T(8,128)(2,1)} %get-tuple-element.6), channel_id=1, source_target_pairs={{2,0},{4,2},{6,4},{8,6},{10,8},{12,10},{14,12},{16,14},{18,16},{20... | collective-permute-start | bytes 73736 | tf_op jit(solution)/shard_map/ppermute | solution.py:29
  152.9 0.6 copy-start.1
  155.2 106.3 %reduce-scatter.5.cloned.1.call-start = ((), (), s32[]{:S(2)}) async-start(), calls=%async_computation.6 | async-start | bytes 98304 | tf_op jit(solution)/shard_map/reduce_scatter | solution.py:115
  180.0 44.8 %all-to-all-start.1 = ((bf16[128,4,128]{2,1,0:T(4,128)(2,1)}), bf16[128,4,128]{2,1,0:T(4,128)(2,1)}, u32[]{:S(2)}, u32[]{:S(2)}) async-start(bf16[128,4,128]{2,1,0:T(4,128)(2,1)} %broadcast_select_fusion.1), calls=%async_computation.2 | async-start | bytes 262144 | tf_op jit(solution)/shard_map/all_to_all | solution.py:131
  206.2 7.0 %copy-start.5 = (s32[3072]{0:T(1024)S(1)}, s32[3072]{0:T(1024)}, u32[]{:S(2)}) copy-start(s32[3072]{0:T(1024)} %pad_clamp_fusion) | copy-start | bytes 36868
  221.5 19.8 %copy-start.6 = (pred[96,27]{1,0:T(8,128)(4,1)S(1)}, pred[96,27]{1,0:T(8,128)(4,1)}, u32[]{:S(2)}) copy-start(pred[96,27]{1,0:T(8,128)(4,1)} %copy.29) | copy-start | bytes 7780
  224.7 32.7 %all-to-all-start.2 = ((bf16[128,4,128]{2,1,0:T(4,128)(2,1)}), bf16[128,4,128]{2,1,0:T(4,128)(2,1)}, u32[]{:S(2)}, u32[]{:S(2)}) async-start(bf16[128,4,128]{2,1,0:T(4,128)(2,1)} %bitcast.215), calls=%async_computation.4 | async-start | bytes 262144 | tf_op jit(solution)/shard_map/all_to_all | solution.py:152
  243.9 3.9 %copy-start.7 = (f32[512,4]{0,1:T(4,128)S(1)}, f32[512,4]{0,1:T(4,128)}, u32[]{:S(2)}) copy-start(f32[512,4]{0,1:T(4,128)} %fusion.28) | copy-start | bytes 24580
  243.9 3.9 %copy-start.3 = (bf16[4,128,256]{1,2,0:T(8,128)(2,1)S(1)}, bf16[4,128,256]{1,2,0:T(8,128)(2,1)}, u32[]{:S(2)}) copy-start(bf16[4,128,256]{1,2,0:T(8,128)(2,1)} %copy.35) | copy-start | bytes 786436
Sparse Core Ops, SparseCore 0:
  155.4 27.0 reduce-scatter.2
  185.2 19.2 reduce-scatter.4
where the time goes:
time: 273 us; the launch traced here: 270 us
  starting transfers between devices  137 us (50%)
  local copies, waits for them, and re-layouts  47.6 us (17%)
  other arithmetic  46.5 us (17%)
  matrix products  14.6 us (5%)
  between operations  14.5 us (5%)
  waiting for transfers between devices  9.16 us (3%)
    ppermute x16, starting transfers between devices, from_behind(): return lax.ppermute(x, axis, pairs)  56 us
    all_to_all x1, starting transfers between devices, on_device(): lax.all_to_all(slot_info, ('cell', 'dir'), split_axis=0, concat_axis=0, t...  25.2 us
    all_to_all x1, starting transfers between devices, on_device(): lax.all_to_all(sent_rows, ('cell', 'dir'), split_axis=0, concat_axis=0, t...  22.4 us
    all_to_all x1, starting transfers between devices, on_device(): lax.all_to_all(replies.reshape(peer_count, slot_count, width_surf), ('cel...  16.6 us
    ppermute x3, starting transfers between devices, swapped(): return lax.ppermute(value, axis, pairs)  12.1 us
    convert_element_type x1, other arithmetic, on_device(): (volume_field.astype(jnp.float32) * contrast_map).astype(jnp.bfloat16)  11.6 us
    gather x2, local copies, waits for them, and re-layouts, on_device(): jnp.take(padded_window, near_ids.reshape(-1), axis=0).reshape(half_rows, -1)  11.6 us
    ppermute x16, waiting for transfers between devices, from_behind(): return lax.ppermute(x, axis, pairs)  5.71 us
  transfers between devices with their start and end apart: 26, of which 4 were waited for; matrix products, arithmetic and copies ran while one was open for 31% of the time, Pallas kernels for 0%

commit v1 on v0

v1 whole, which is shorter than its diff:
```python
import jax
import jax.numpy as jnp
from jax import lax
from jax.experimental import pallas as pl
from jax.experimental.pallas import tpu as pltpu
from jax.sharding import PartitionSpec as P

MESH = pl.DeviceIdType.MESH
F32 = jnp.float32
BF16 = jnp.bfloat16

NX = 4
NZ = 16
NY = 4
NJ = 8
NCELL = NZ * NY
CAP = 4
KINDS = 4
LC = 192
HALF = 96
LS = 128
HW = 48
NN = 27
VX = 256
KH = 128
WIN = 384


def dot(a, b, ca=1, cb=0):
    return lax.dot_general(a, b, (((ca,), (cb,)), ((), ())), preferred_element_type=F32)


def onehot(mask):
    return jnp.where(mask, 1.0, 0.0).astype(BF16)


def iota(shape, dim):
    return lax.broadcasted_iota(jnp.int32, shape, dim)


class Exchange:
    def __init__(self, count, me, device, src, dst, send, recv):
        self.count, self.me, self.device = count, me, device
        self.src, self.dst, self.send, self.recv = src, dst, send, recv

    def copy(self, step, slot):
        target = lax.rem(self.me + step, self.count)
        return pltpu.make_async_remote_copy(
            src_ref=self.src(target),
            dst_ref=self.dst.at[slot],
            send_sem=self.send.at[step],
            recv_sem=self.recv.at[step],
            device_id=self.device(target),
            device_id_type=MESH,
        )

    def loop(self, body):
        def wrapped(step, carry):
            body(step)
            return carry

        lax.fori_loop(1, self.count, wrapped, 0)

    def start(self):
        self.loop(lambda step: self.copy(step, self.me).start())

    def wait_recv(self):
        def body(step):
            source = lax.rem(self.me + self.count - step, self.count)
            self.copy(step, source).wait_recv()

        self.loop(body)

    def wait_send(self):
        self.loop(lambda step: self.copy(step, self.me).wait_send())


def kernel(
    vf, cid, con, near_t, nb_hbm, vrad, srad, vrec, srec, cur, host, lout, lin, tab, sv, pt,
    vout, sout,
    nb, win, halo, msg_info, in_info, mid_info2, all_info,
    msg_cur, in_cur, f_rows, mid_cur, all_cur,
    table, rep_a, rep_b, rep_c, rep_d,
    crow, in_c, mid_c, all_c, up0, xrows, up1, up2, up3,
    lins, tabs, idx_pad, gathered,
    z_send, z_recv, j_send, j_recv, p_send, p_recv, nb_sem,
):
    x = lax.axis_index("sec")
    cell = lax.axis_index("cell")
    c = lax.axis_index("dir")
    z = lax.div(cell, NY)
    y = lax.rem(cell, NY)
    j = y * 2 + c
    g = x * NCELL + cell

    nb_copy = pltpu.make_async_copy(nb_hbm, nb, nb_sem)
    nb_copy.start()

    def z_device(other):
        return (x, other * NY + y, c)

    def j_device(other):
        return (x, z * NY + lax.div(other, 2), lax.rem(other, 2))

    def g_device(step):
        other = lax.rem(g + step + NX * NCELL, NX * NCELL)
        return (lax.div(other, NCELL), lax.rem(other, NCELL), c)

    def x_device(step):
        return (lax.rem(x + step + NX, NX), cell, c)

    barrier = pltpu.get_barrier_semaphore()

    def greet(device):
        pl.semaphore_signal(barrier, inc=1, device_id=device, device_id_type=MESH)

    def greet_z(step, carry):
        greet(z_device(lax.rem(z + step, NZ)))
        return carry

    def greet_j(step, carry):
        greet(j_device(lax.rem(j + step, NJ)))
        return carry

    lax.fori_loop(1, NZ, greet_z, 0)
    lax.fori_loop(1, NJ, greet_j, 0)
    for step in (-1, 1):
        greet(g_device(step))
        greet(x_device(step))

    z_info = Exchange(NZ, z, z_device, lambda t: msg_info.at[t], in_info, z_send.at[0], z_recv.at[0])
    z_cur = Exchange(NZ, z, z_device, lambda t: msg_cur.at[t], in_cur, z_send.at[1], z_recv.at[1])
    z_tree = Exchange(NZ, z, z_device, lambda t: crow, in_c, z_send.at[2], z_recv.at[2])
    z_rep = Exchange(NZ, z, z_device, lambda t: rep_c.at[t], rep_d, z_send.at[3], z_recv.at[3])
    j_info = Exchange(NJ, j, j_device, lambda t: mid_info2, all_info, j_send.at[0], j_recv.at[0])
    j_cur = Exchange(NJ, j, j_device, lambda t: mid_cur.at[t], all_cur, j_send.at[1], j_recv.at[1])
    j_tree = Exchange(NJ, j, j_device, lambda t: mid_c, all_c, j_send.at[2], j_recv.at[2])
    j_rep = Exchange(NJ, j, j_device, lambda t: rep_a.at[t], rep_b, j_send.at[3], j_recv.at[3])

    def pair_copy(number, src, dst, device):
        return pltpu.make_async_remote_copy(
            src_ref=src,
            dst_ref=dst,
            send_sem=p_send.at[number],
            recv_sem=p_recv.at[number],
            device_id=device,
            device_id_type=MESH,
        )

    other_core = (x, cell, 1 - c)
    lin_copy = pair_copy(0, lin, lins.at[c], other_core)
    tab_copy = pair_copy(1, tab, tabs.at[c], other_core)
    halo_right = pair_copy(2, win.at[pl.ds(LC, HW)], halo.at[0], g_device(1))
    halo_left = pair_copy(3, win.at[pl.ds(HW, HW)], halo.at[1], g_device(-1))
    x_right = pair_copy(4, up0.at[:, pl.ds(NCELL, 32)], xrows.at[0], x_device(1))
    x_left = pair_copy(5, up0.at[:, pl.ds(32, 32)], xrows.at[1], x_device(-1))

    with jax.named_scope("pairs_out"):
        rows = [pt[f].astype(F32) for f in range(3)]
        rows = jnp.concatenate(rows + [jnp.zeros((CAP, LS), F32)], axis=0)
        columns = jnp.transpose(rows)
        lane = iota((LS, LS), 1)
        row_low = iota((LS, LS), 0) & (NJ - 1)
        info = jnp.zeros((LS, LS), F32)
        for slot in range(CAP):
            for field in range(2):
                hit = lane == row_low + (field * 32 + slot * NJ)
                info = info + jnp.where(hit, columns[:, 4 + 4 * field + slot][:, None], 0.0)
        spread = onehot((iota((NZ, LS), 1) >> 3) == iota((NZ, LS), 0))
        info = dot(spread, info.astype(BF16))
        for t in range(NZ):
            msg_info[t] = info[t : t + 1]
        own = cur[pl.ds(pl.multiple_of(c * 64, 64), 64), :]
        lane64 = iota((LS, 64), 1).astype(F32)
        parts = []
        for slot in range(CAP):
            pick = onehot(columns[:, slot : slot + 1] == lane64)
            parts.append(dot(pick, own).reshape(NZ, NJ, LS))
        msg_cur[...] = jnp.concatenate(parts, axis=1).astype(BF16)

    pl.semaphore_wait(barrier, (NZ - 1) + (NJ - 1) + 4)
    z_info.start()
    lin_copy.start()
    tab_copy.start()
    z_cur.start()
    in_info[pl.ds(z, 1)] = msg_info[pl.ds(z, 1)]
    in_cur[pl.ds(z, 1)] = msg_cur[pl.ds(z, 1)]
    lins[pl.ds(c, 1)] = lin[...][None]
    tabs[pl.ds(c, 1)] = tab[...][None]

    with jax.named_scope("weighted"):
        ids = cid[...]
        scale = jnp.zeros((LC, VX), F32)
        for m in range(16):
            scale = jnp.where(ids == m, con[m], scale)
        win[pl.ds(HW, LC), :] = (vf[...].astype(F32) * scale).astype(BF16)
    halo_right.start()
    halo_left.start()

    with jax.named_scope("coarse"):
        weighted = win[pl.ds(HW, LC), :]
        outgoing = dot(weighted, vrad[...])
        surf_waves = dot(cur[...], srad[...])
        host_t = onehot(host[...] == iota((LC, LS), 0))
        leaf = lout[...]
        leaf_surf = dot(host_t, leaf, 0, 0)
        coarse = jnp.sum(leaf.astype(F32) * outgoing, axis=0, keepdims=True)
        coarse = coarse + jnp.sum(leaf_surf * surf_waves, axis=0, keepdims=True)
        crow[...] = coarse
    z_tree.start()
    in_c[pl.ds(z, 1)] = crow[...][None]

    with jax.named_scope("reply_table"):
        own_weighted = win[pl.ds(pl.multiple_of(HW + c * HALF, 16), HALF), :]
        for kind in range(KINDS):
            table[pl.ds(kind * HALF, HALF), :] = dot(own_weighted, sv[kind], 1, 1).astype(BF16)

    z_info.wait_recv()
    for t in range(NZ):
        mid_info2[pl.ds(t, 1), :] = in_info[t]
    j_info.start()
    all_info[pl.ds(j, 1)] = mid_info2[...][None]

    z_tree.wait_recv()
    for t in range(NZ):
        mid_c[pl.ds(t, 1), :] = in_c[t]
    j_tree.start()
    all_c[pl.ds(j, 1)] = mid_c[...][None]

    j_info.wait_recv()
    with jax.named_scope("replies"):
        codes = all_info[...].reshape(LS, LS)
        codes = pltpu.roll(codes, lax.rem(LS - j, LS), 1)
        lane384 = iota((LS, KINDS * HALF), 1).astype(F32)
        picks = []
        for slot in range(CAP):
            at = slot * NJ
            code = codes[:, at : at + 1] + HALF * codes[:, 32 + at : 33 + at]
            pick = onehot(code == lane384)
            picks.append(pick)
            rep = dot(pick, table[...]).astype(BF16)
            rep_a[:, slot] = rep.reshape(NJ, NZ, LS)
    j_rep.start()
    rep_b[pl.ds(j, 1)] = rep_a[pl.ds(j, 1)]

    j_tree.wait_recv()
    with jax.named_scope("section_rows"):
        for yy in range(NY):
            for cc in range(2):
                up0[cc, pl.ds(32 + yy, NZ, stride=NY), :] = all_c[2 * yy + cc]
    x_right.start()
    x_left.start()

    z_cur.wait_recv()
    with jax.named_scope("regroup_currents"):
        f_rows[...] = in_cur[...].astype(F32).reshape(NZ * 32, LS)
        for jj in range(NJ):
            for slot in range(CAP):
                block = f_rows[pl.ds(slot * NJ + jj, NZ, stride=32), :]
                mid_cur[jj, slot] = block.astype(BF16)
    j_cur.start()
    all_cur[pl.ds(j, 1)] = mid_cur[pl.ds(j, 1)]

    j_rep.wait_recv()
    with jax.named_scope("regroup_replies"):
        f_rows[...] = rep_b[...].astype(F32).reshape(NJ * 64, LS)
        for zz in range(NZ):
            blocks = [f_rows[pl.ds(slot * NZ + zz, NJ, stride=64), :] for slot in range(CAP)]
            rep_c[zz] = jnp.concatenate(blocks, axis=0).astype(BF16)
    z_rep.start()
    rep_d[pl.ds(z, 1)] = rep_c[pl.ds(z, 1)]

    halo_right.wait_recv()
    halo_left.wait_recv()
    nb_copy.wait()
    with jax.named_scope("near"):
        first = jnp.where(g > 0, 1.0, 0.0)
        last = jnp.where(g < NX * NCELL - 1, 1.0, 0.0)
        win[pl.ds(0, HW), :] = jnp.where(first > 0.5, halo[0].astype(F32), 0.0).astype(BF16)
        win[pl.ds(HW + LC, HW), :] = jnp.where(last > 0.5, halo[1].astype(F32), 0.0).astype(BF16)
        win[pl.ds(2 * HW + LC, WIN - 2 * HW - LC), :] = jnp.zeros((WIN - 2 * HW - LC, VX), BF16)
        idx_pad[...] = jnp.zeros((32, 128), F32)
        idx_pad[pl.ds(0, NN), pl.ds(0, HALF)] = near_t[...].astype(F32)
        slots = jnp.transpose(idx_pad[...])[:HALF]
        lane_w = iota((HALF, WIN), 1).astype(F32)
        window = win[...]
        for n in range(NN):
            pick = onehot(slots[:, n : n + 1] == lane_w)
            gathered[n] = dot(pick, window).astype(BF16)
        near = jnp.zeros((HALF, VX), F32)
        for n in range(NN):
            near = near + dot(gathered[n], nb[n])

    j_cur.wait_recv()
    with jax.named_scope("coupled_volume"):
        sums = jnp.zeros((KINDS * HALF, LS), F32)
        for slot in range(CAP):
            sums = sums + dot(picks[slot], all_cur[:, slot].reshape(LS, LS), 0, 0)
        high = sums.astype(BF16)
        low = (sums - high.astype(F32)).astype(BF16)
        coupled = jnp.zeros((HALF, VX), F32)
        for kind in range(KINDS):
            part = slice(kind * HALF, (kind + 1) * HALF)
            coupled = coupled + dot(high[part], sv[kind]) + dot(low[part], sv[kind])

    x_right.wait_recv()
    x_left.wait_recv()
    tab_copy.wait_recv()
    with jax.named_scope("tree"):
        up0[:, pl.ds(0, 32), :] = jnp.where(x > 0, xrows[0], 0.0)
        up0[:, pl.ds(96, 32), :] = jnp.where(x < NX - 1, xrows[1], 0.0)
        ups = [up0, up1, up2, up3]
        waves = []
        for h in range(2):

            def entry(level, number):
                return tabs[h, level, pl.ds(number, 1), :]

            for level in range(3):
                count = 64 >> level
                even = ups[level][h, pl.ds(0, count, stride=2), :]
                odd = ups[level][h, pl.ds(1, count, stride=2), :]
                ups[level + 1][h] = entry(level, 4) * even + entry(level, 5) * odd
            terms = []
            for level in range(4):
                at = (32 + cell) >> level
                is_odd = (at & 1) == 1

                def row(offset):
                    return ups[level][h, pl.ds(at + offset, 1), :]

                term = jnp.where(is_odd, entry(level, 0) * row(-3), 0.0)
                term = term + entry(level, 1) * row(-2)
                term = term + entry(level, 2) * row(2)
                term = term + jnp.where(is_odd, 0.0, entry(level, 3) * row(3))
                terms.append(term)
            down = terms[3]
            for level in (2, 1, 0):
                is_odd = (((32 + cell) >> level) & 1) == 1
                down = terms[level] + jnp.where(is_odd, entry(level, 7), entry(level, 6)) * down
            waves.append(down)

    lin_copy.wait_recv()
    with jax.named_scope("far"):
        far_volume = jnp.zeros((HALF, VX), F32)
        far_surface = jnp.zeros((64, LS), F32)
        for h in range(2):
            wave = waves[h]
            leaf_own = lins[h, pl.ds(pl.multiple_of(c * HALF, 32), HALF), :].astype(F32)
            incoming = (leaf_own * wave).astype(BF16)
            far_volume = far_volume + dot(incoming, vrec[pl.ds(h * KH, KH), :])
            leaf_all = dot(host_t, lins[h], 0, 0)
            leaf_here = jnp.where(c == 0, leaf_all[:64], leaf_all[64:])
            incoming = (leaf_here * wave).astype(BF16)
            far_surface = far_surface + dot(incoming, srec[pl.ds(h * KH, KH), :])
        field = vf[pl.ds(pl.multiple_of(c * HALF, 32), HALF), :].astype(F32)
        vout[...] = field + near + far_volume + coupled

    z_rep.wait_recv()
    with jax.named_scope("coupled_surface"):
        back = rep_d[...].astype(F32)
        sublane64 = iota((64, LS), 0)
        total = far_surface
        for slot in range(CAP):
            pick = onehot(pt[0, pl.ds(slot, 1), :] == sublane64)
            mine = back[:, slot * NJ : (slot + 1) * NJ, :].reshape(LS, LS).astype(BF16)
            total = total + dot(pick, mine)
        sout[...] = total

    for exchange in (z_info, z_cur, z_tree, z_rep, j_info, j_cur, j_tree, j_rep):
        exchange.wait_send()
    for copy in (lin_copy, tab_copy, halo_right, halo_left, x_right, x_left):
        copy.wait_send()


def on_device(
    volume_field, contrast_id, contrast, near_index, near_blocks, vol_radiation, surf_radiation,
    vol_receive, surf_receive, surface_current, surf_host, leaf_out, leaf_in, level_tables,
    sv_blocks, pair_table,
):
    vmem = pl.BlockSpec(memory_space=pltpu.VMEM)
    specs = [vmem] * 16
    specs[2] = pl.BlockSpec(memory_space=pltpu.SMEM)
    specs[4] = pl.BlockSpec(memory_space=pl.ANY)
    return pl.pallas_call(
        kernel,
        out_shape=(
            jax.ShapeDtypeStruct((HALF, VX), F32),
            jax.ShapeDtypeStruct((64, LS), F32),
        ),
        in_specs=specs,
        out_specs=(vmem, vmem),
        scratch_shapes=[
            pltpu.VMEM((NN, VX, VX), BF16),
            pltpu.VMEM((WIN, VX), BF16),
            pltpu.VMEM((2, HW, VX), BF16),
            pltpu.VMEM((NZ, 1, LS), F32),
            pltpu.VMEM((NZ, 1, LS), F32),
            pltpu.VMEM((NZ, LS), F32),
            pltpu.VMEM((NJ, NZ, LS), F32),
            pltpu.VMEM((NZ, 32, LS), BF16),
            pltpu.VMEM((NZ, 32, LS), BF16),
            pltpu.VMEM((512, LS), F32),
            pltpu.VMEM((NJ, CAP, NZ, LS), BF16),
            pltpu.VMEM((NJ, CAP, NZ, LS), BF16),
            pltpu.VMEM((KINDS * HALF, LS), BF16),
            pltpu.VMEM((NJ, CAP, NZ, LS), BF16),
            pltpu.VMEM((NJ, CAP, NZ, LS), BF16),
            pltpu.VMEM((NZ, 32, LS), BF16),
            pltpu.VMEM((NZ, 32, LS), BF16),
            pltpu.VMEM((1, KH), F32),
            pltpu.VMEM((NZ, 1, KH), F32),
            pltpu.VMEM((NZ, KH), F32),
            pltpu.VMEM((NJ, NZ, KH), F32),
            pltpu.VMEM((2, 128, KH), F32),
            pltpu.VMEM((2, 2, 32, KH), F32),
            pltpu.VMEM((2, 64, KH), F32),
            pltpu.VMEM((2, 32, KH), F32),
            pltpu.VMEM((2, 16, KH), F32),
            pltpu.VMEM((2, LC, KH), BF16),
            pltpu.VMEM((2, 4, 8, KH), F32),
            pltpu.VMEM((32, 128), F32),
            pltpu.VMEM((NN, HALF, VX), BF16),
            pltpu.SemaphoreType.DMA((4, NZ)),
            pltpu.SemaphoreType.DMA((4, NZ)),
            pltpu.SemaphoreType.DMA((4, NJ)),
            pltpu.SemaphoreType.DMA((4, NJ)),
            pltpu.SemaphoreType.DMA((6,)),
            pltpu.SemaphoreType.DMA((6,)),
            pltpu.SemaphoreType.DMA,
        ],
        compiler_params=pltpu.CompilerParams(
            collective_id=0, has_side_effects=True, vmem_limit_bytes=40 * 1024 * 1024
        ),
    )(
        volume_field, contrast_id, contrast, near_index.T, near_blocks, vol_radiation,
        surf_radiation, vol_receive, surf_receive, surface_current, surf_host.reshape(1, LS),
        leaf_out, leaf_in, level_tables, sv_blocks, jnp.transpose(pair_table, (2, 1, 0)),
    )


def solution(mesh):
    in_specs = (
        P(("sec", "cell"), None),
        P(("sec", "cell"), None),
        P(),
        P(("sec", "cell", "dir"), None),
        P(),
        P(None, "dir"),
        P(None, "dir"),
        P(),
        P(),
        P(("sec", "cell"), None),
        P(("sec", "cell")),
        P(None, "dir"),
        P(None, "dir"),
        P(None, None, "dir"),
        P(),
        P(("sec", "cell", "dir"), None, None),
    )
    out_specs = (P(("sec", "cell", "dir"), None), P(("sec", "cell", "dir"), None))
    return jax.shard_map(
        on_device, mesh=mesh, in_specs=in_specs, out_specs=out_specs, check_vma=False
    )
```

time: 273 us -> 64 us (0.23)
  starting transfers between devices: 137 us -> 0 us
  Pallas kernels: 0 us -> 47.4 us
  other arithmetic: 46.5 us -> 0 us
  local copies, waits for them, and re-layouts: 47.6 us -> 15.1 us
  matrix products: 14.6 us -> 0 us
  between operations: 14.5 us -> 0.67 us
  waiting for transfers between devices: 9.16 us -> 0 us
    ppermute x21 -> x0, starting transfers between devices: 73.1 us -> none  [the longest x16 56 us: from_behind(): return lax.ppermute(x, axis, pairs)]
    all_to_all x3 -> x0, starting transfers between devices: 64.2 us -> none  [the longest x1 25.2 us: on_device(): lax.all_to_all(slot_info, ('cell', 'dir'), split_axis=0, concat_axis=0, t...]
    pallas_call x0 -> x1, Pallas kernels: none -> 47.4 us  [on_device(): pl.pallas_call(kernel, out_shape=(jax.ShapeDtypeStruct((HALF, VX), F32),...]
    gather x5 -> x0, local copies, waits for them, and re-layouts: 19.4 us -> none  [the longest x2 11.6 us: on_device(): jnp.take(padded_window, near_ids.reshape(-1), axis=0).reshape(half_rows, -1)]
    dot_general x7 -> x0, matrix products: 14.6 us -> none  [the longest x1 3.85 us: on_device(): jnp.dot(gathered, near_blocks.reshape(-1, width_vol), preferred_element_t...]
    convert_element_type x3 -> x0, other arithmetic: 13 us -> none  [the longest x1 11.6 us: on_device(): (volume_field.astype(jnp.float32) * contrast_map).astype(jnp.bfloat16)]
    scatter-add x3 -> x0, other arithmetic: 12.1 us -> none  [the longest x1 5.01 us: on_device(): jax.ops.segment_sum(pushed.reshape(-1, width_vol), cell_ids.reshape(-1),...]
    unnamed x29 -> x34, local copies, waits for them, and re-layouts: 4.1 us -> 15.1 us
  transfers between devices with their start and end apart: 26 -> 0, of which waited for: 4 -> 0; matrix products, arithmetic and copies ran while one was open for 31% -> 0% of each run, Pallas kernels for 0% -> 0%
where the time goes in v1:
time: 64 us; the launch traced here: 63.3 us
  Pallas kernels  47.4 us (74%)
  local copies, waits for them, and re-layouts  15.1 us (24%)
  between operations  0.67 us (1%)
    pallas_call x1, Pallas kernels, on_device(): pl.pallas_call(kernel, out_shape=(jax.ShapeDtypeStruct((HALF, VX), F32),...  47.4 us
    unnamed x34, local copies, waits for them, and re-layouts  15.1 us

profile of v1, /device:TPU:1, one launch (start us, length us, event | category | flops | bytes accessed | tf_op | source)
XLA Modules:
  0.0 63.3 jit_solution(2810419367771880233)
XLA Ops:
  0.6 0.0 copy-start
  0.6 2.0 %copy-done = bf16[27,256,256]{2,1,0:T(8,128)(2,1)S(1)} copy-done((bf16[27,256,256]{2,1,0:T(8,128)(2,1)S(1)}, bf16[27,256,256]{2,1,0:T(8,128)(2,1)}, u32[]{:S(2)}) %copy-start) | copy-done | bytes 3538968
  2.6 0.0 copy-start.1
  2.6 0.9 %copy-done.1 = bf16[4,128,256]{2,1,0:T(8,128)(2,1)S(1)} copy-done((bf16[4,128,256]{2,1,0:T(8,128)(2,1)S(1)}, bf16[4,128,256]{2,1,0:T(8,128)(2,1)}, u32[]{:S(2)}) %copy-start.1) | copy-done | bytes 262168
  3.6 0.0 copy-start.2
  3.6 0.9 %copy-done.2 = s32[192,256]{1,0:T(8,128)S(1)} copy-done((s32[192,256]{1,0:T(8,128)S(1)}, s32[192,256]{1,0:T(8,128)}, u32[]{:S(2)}) %copy-start.2) | copy-done | bytes 196632
  4.5 0.0 copy-start.3
  4.5 0.9 %copy-done.3 = bf16[256,256]{1,0:T(8,128)(2,1)S(1)} copy-done((bf16[256,256]{1,0:T(8,128)(2,1)S(1)}, bf16[256,256]{1,0:T(8,128)(2,1)}, u32[]{:S(2)}) %copy-start.3) | copy-done | bytes 131096
  5.4 0.0 copy-start.4
  5.4 0.9 %copy-done.4 = bf16[192,256]{1,0:T(8,128)(2,1)S(1)} copy-done((bf16[192,256]{1,0:T(8,128)(2,1)S(1)}, bf16[192,256]{1,0:T(8,128)(2,1)}, u32[]{:S(2)}) %copy-start.4) | copy-done | bytes 98328
  6.3 0.0 copy-start.5
  6.3 0.8 %copy-done.5 = bf16[256,128]{1,0:T(8,128)(2,1)S(1)} copy-done((bf16[256,128]{1,0:T(8,128)(2,1)S(1)}, bf16[256,128]{1,0:T(8,128)(2,1)}, u32[]{:S(2)}) %copy-start.5) | copy-done | bytes 65560
  7.2 0.0 copy-start.6
  7.2 0.8 %copy-done.6 = bf16[256,128]{1,0:T(8,128)(2,1)S(1)} copy-done((bf16[256,128]{1,0:T(8,128)(2,1)S(1)}, bf16[256,128]{1,0:T(8,128)(2,1)}, u32[]{:S(2)}) %copy-start.6) | copy-done | bytes 65560
  8.0 0.0 copy-start.7
  8.0 0.8 %copy-done.7 = bf16[192,128]{1,0:T(8,128)(2,1)S(1)} copy-done((bf16[192,128]{1,0:T(8,128)(2,1)S(1)}, bf16[192,128]{1,0:T(8,128)(2,1)}, u32[]{:S(2)}) %copy-start.7) | copy-done | bytes 49176
  8.8 0.0 copy-start.8
  8.8 0.8 %copy-done.8 = bf16[192,128]{1,0:T(8,128)(2,1)S(1)} copy-done((bf16[192,128]{1,0:T(8,128)(2,1)S(1)}, bf16[192,128]{1,0:T(8,128)(2,1)}, u32[]{:S(2)}) %copy-start.8) | copy-done | bytes 49176
  9.6 0.0 copy-start.9
  9.6 0.8 %copy-done.9 = bf16[128,128]{1,0:T(8,128)(2,1)S(1)} copy-done((bf16[128,128]{1,0:T(8,128)(2,1)S(1)}, bf16[128,128]{1,0:T(8,128)(2,1)}, u32[]{:S(2)}) %copy-start.9) | copy-done | bytes 32792
  10.4 0.0 copy-start.10
  10.4 0.8 %copy-done.10 = bf16[128,128]{1,0:T(8,128)(2,1)S(1)} copy-done((bf16[128,128]{1,0:T(8,128)(2,1)S(1)}, bf16[128,128]{1,0:T(8,128)(2,1)}, u32[]{:S(2)}) %copy-start.10) | copy-done | bytes 32792
  11.1 0.0 copy-start.11
  11.1 0.7 %copy-done.11 = s32[96,27]{0,1:T(8,128)S(1)} copy-done((s32[96,27]{0,1:T(8,128)S(1)}, s32[96,27]{0,1:T(8,128)}, u32[]{:S(2)}) %copy-start.11) | copy-done | bytes 10392
  11.8 0.0 copy-start.12
  11.8 0.7 %copy-done.12 = f32[4,8,128]{2,1,0:T(8,128)S(1)} copy-done((f32[4,8,128]{2,1,0:T(8,128)S(1)}, f32[4,8,128]{2,1,0:T(8,128)}, u32[]{:S(2)}) %copy-start.12) | copy-done | bytes 16408
  12.5 0.0 copy-start.13
  12.5 0.7 %copy-done.13 = s32[128,4,3]{0,1,2:T(4,128)S(1)} copy-done((s32[128,4,3]{0,1,2:T(4,128)S(1)}, s32[128,4,3]{0,1,2:T(4,128)}, u32[]{:S(2)}) %copy-start.13) | copy-done | bytes 6168
  13.2 0.0 copy-start.14
  13.2 0.7 %copy-done.14 = f32[16]{0:T(128)S(1)} copy-done((f32[16]{0:T(128)S(1)}, f32[16]{0:T(128)}, u32[]{:S(2)}) %copy-start.14) | copy-done | bytes 88
  13.9 0.0 copy-start.15
  13.9 0.7 %copy-done.15 = s32[128]{0:T(128)S(1)} copy-done((s32[128]{0:T(128)S(1)}, s32[128]{0:T(128)}, u32[]{:S(2)}) %copy-start.15) | copy-done | bytes 536
  14.5 47.4 %shard_map.167 = (f32[96,256]{1,0:T(8,128)S(1)}, f32[64,128]{1,0:T(8,128)S(1)}) custom-call(bf16[192,256]{1,0:T(8,128)(2,1)S(1)} %copy-done.4, s32[192,256]{1,0:T(8,128)S(1)} %copy-done.2, f32[16]{0:T(128)S(1)} %copy-done.14, s32[27,96]{1,0:T(8,128)S(1)} %bitcast.3, bf16[27,256,256]{2,1,0:T(8,128)(2,1)S(1)} %copy-done, bf16[256,128]{1,0:T(8,128)(2,1)S(1)} %copy-done.5, ...), custom_call_target="tpu_custom_call" | custom-call | tf_op jit(solution)/shard_map/pallas_call | solution.py:385
  62.0 0.6 %copy.20 = f32[96,256]{1,0:T(8,128)} copy(f32[96,256]{1,0:T(8,128)S(1)} %get-tuple-element.4) | data formatting | bytes 196608
  62.6 0.6 copy.21
Async XLA Ops:
  0.6 2.0 %copy-start = (bf16[27,256,256]{2,1,0:T(8,128)(2,1)S(1)}, bf16[27,256,256]{2,1,0:T(8,128)(2,1)}, u32[]{:S(2)}) copy-start(bf16[27,256,256]{2,1,0:T(8,128)(2,1)} %nb_hbm.1) | copy-start | bytes 10616836
  2.6 0.9 %copy-start.1 = (bf16[4,128,256]{2,1,0:T(8,128)(2,1)S(1)}, bf16[4,128,256]{2,1,0:T(8,128)(2,1)}, u32[]{:S(2)}) copy-start(bf16[4,128,256]{2,1,0:T(8,128)(2,1)} %sv.1) | copy-start | bytes 786436
  3.6 0.9 %copy-start.2 = (s32[192,256]{1,0:T(8,128)S(1)}, s32[192,256]{1,0:T(8,128)}, u32[]{:S(2)}) copy-start(s32[192,256]{1,0:T(8,128)} %cid.1) | copy-start | bytes 589828
  4.5 0.9 %copy-start.3 = (bf16[256,256]{1,0:T(8,128)(2,1)S(1)}, bf16[256,256]{1,0:T(8,128)(2,1)}, u32[]{:S(2)}) copy-start(bf16[256,256]{1,0:T(8,128)(2,1)} %vrec.1) | copy-start | bytes 393220
  5.4 0.9 %copy-start.4 = (bf16[192,256]{1,0:T(8,128)(2,1)S(1)}, bf16[192,256]{1,0:T(8,128)(2,1)}, u32[]{:S(2)}) copy-start(bf16[192,256]{1,0:T(8,128)(2,1)} %vf.1) | copy-start | bytes 294916
  6.3 0.8 %copy-start.5 = (bf16[256,128]{1,0:T(8,128)(2,1)S(1)}, bf16[256,128]{1,0:T(8,128)(2,1)}, u32[]{:S(2)}) copy-start(bf16[256,128]{1,0:T(8,128)(2,1)} %vrad.1) | copy-start | bytes 196612
  7.2 0.8 %copy-start.6 = (bf16[256,128]{1,0:T(8,128)(2,1)S(1)}, bf16[256,128]{1,0:T(8,128)(2,1)}, u32[]{:S(2)}) copy-start(bf16[256,128]{1,0:T(8,128)(2,1)} %srec.1) | copy-start | bytes 196612
  8.0 0.8 %copy-start.7 = (bf16[192,128]{1,0:T(8,128)(2,1)S(1)}, bf16[192,128]{1,0:T(8,128)(2,1)}, u32[]{:S(2)}) copy-start(bf16[192,128]{1,0:T(8,128)(2,1)} %lout.1) | copy-start | bytes 147460
  8.8 0.8 %copy-start.8 = (bf16[192,128]{1,0:T(8,128)(2,1)S(1)}, bf16[192,128]{1,0:T(8,128)(2,1)}, u32[]{:S(2)}) copy-start(bf16[192,128]{1,0:T(8,128)(2,1)} %lin.1) | copy-start | bytes 147460
  9.6 0.8 %copy-start.9 = (bf16[128,128]{1,0:T(8,128)(2,1)S(1)}, bf16[128,128]{1,0:T(8,128)(2,1)}, u32[]{:S(2)}) copy-start(bf16[128,128]{1,0:T(8,128)(2,1)} %srad.1) | copy-start | bytes 98308
  10.4 0.8 %copy-start.10 = (bf16[128,128]{1,0:T(8,128)(2,1)S(1)}, bf16[128,128]{1,0:T(8,128)(2,1)}, u32[]{:S(2)}) copy-start(bf16[128,128]{1,0:T(8,128)(2,1)} %cur.1) | copy-start | bytes 98308
  11.1 0.7 %copy-start.11 = (s32[96,27]{0,1:T(8,128)S(1)}, s32[96,27]{0,1:T(8,128)}, u32[]{:S(2)}) copy-start(s32[96,27]{0,1:T(8,128)} %param.19) | copy-start | bytes 31108
  11.8 0.7 %copy-start.12 = (f32[4,8,128]{2,1,0:T(8,128)S(1)}, f32[4,8,128]{2,1,0:T(8,128)}, u32[]{:S(2)}) copy-start(f32[4,8,128]{2,1,0:T(8,128)} %tab.1) | copy-start | bytes 49156
  12.5 0.7 %copy-start.13 = (s32[128,4,3]{0,1,2:T(4,128)S(1)}, s32[128,4,3]{0,1,2:T(4,128)}, u32[]{:S(2)}) copy-start(s32[128,4,3]{0,1,2:T(4,128)} %param.31) | copy-start | bytes 18436
  13.2 0.7 %copy-start.14 = (f32[16]{0:T(128)S(1)}, f32[16]{0:T(128)}, u32[]{:S(2)}) copy-start(f32[16]{0:T(128)} %con.1) | copy-start | bytes 196
  13.9 0.7 %copy-start.15 = (s32[128]{0:T(128)S(1)}, s32[128]{0:T(128)}, u32[]{:S(2)}) copy-start(s32[128]{0:T(128)} %param.26) | copy-start | bytes 1540

commit v2 on v1

--- a/solution.py
+++ b/solution.py
@@ -44,7 +44,7 @@
         self.src, self.dst, self.send, self.recv = src, dst, send, recv
 
     def copy(self, step, slot):
-        target = lax.rem(self.me + step, self.count)
+        target = lax.rem(self.me + self.offset(step), self.count)
         return pltpu.make_async_remote_copy(
             src_ref=self.src(target),
             dst_ref=self.dst.at[slot],
@@ -54,6 +54,10 @@
             device_id_type=MESH,
         )
 
+    def offset(self, step):
+        low = lax.div(self.count + 1 - step, 2)
+        return jnp.where(lax.rem(step, 2) == 1, low, self.count - low)
+
     def loop(self, body):
         def wrapped(step, carry):
             body(step)
@@ -66,7 +70,7 @@
 
     def wait_recv(self):
         def body(step):
-            source = lax.rem(self.me + self.count - step, self.count)
+            source = lax.rem(self.me + self.count - self.offset(step), self.count)
             self.copy(step, source).wait_recv()
 
         self.loop(body)
@@ -76,14 +80,15 @@
 
 
 def kernel(
-    vf, cid, con, near_t, nb_hbm, vrad, srad, vrec, srec, cur, host, lout, lin, tab, sv, pt,
+    vf_in, cid_in, con_in, near_in, nb_in, vrad_in, srad_in, vrec_in, srec_in, cur_in, host_in,
+    lout_in, lin_in, tab_in, sv_in, pt_in,
     vout, sout,
-    nb, win, halo, msg_info, in_info, mid_info2, all_info,
+    vf, cid, con, near_t, nb, vrad, srad, vrec, srec, cur, host, lout, sv, pt, win, halo, msg, in_info, mid_info, all_info, crow, in_c, mid_c, all_c,
     msg_cur, in_cur, f_rows, mid_cur, all_cur,
     table, rep_a, rep_b, rep_c, rep_d,
-    crow, in_c, mid_c, all_c, up0, xrows, up1, up2, up3,
+    up0, xrows, up1, up2, up3,
     lins, tabs, idx_pad, gathered,
-    z_send, z_recv, j_send, j_recv, p_send, p_recv, nb_sem,
+    z_send, z_recv, j_send, j_recv, p_send, p_recv, load_sem,
 ):
     x = lax.axis_index("sec")
     cell = lax.axis_index("cell")
@@ -93,8 +98,21 @@
     j = y * 2 + c
     g = x * NCELL + cell
 
-    nb_copy = pltpu.make_async_copy(nb_hbm, nb, nb_sem)
-    nb_copy.start()
+    loads = {}
+    order = [
+        ("pt", pt_in, pt), ("cur", cur_in, cur), ("cid", cid_in, cid), ("vf", vf_in, vf),
+        ("con", con_in, con), ("vrad", vrad_in, vrad), ("srad", srad_in, srad),
+        ("host", host_in, host), ("lout", lout_in, lout), ("sv", sv_in, sv),
+        ("near", near_in, near_t), ("lin", lin_in, lins.at[c]), ("tab", tab_in, tabs.at[c]),
+        ("nb", nb_in, nb), ("vrec", vrec_in, vrec), ("srec", srec_in, srec),
+    ]
+    for number, (name, src, dst) in enumerate(order):
+        loads[name] = pltpu.make_async_copy(src, dst, load_sem.at[number])
+    loads["pt"].start()
+
+    def loaded(*names):
+        for name in names:
+            loads[name].wait()
 
     def z_device(other):
         return (x, other * NY + y, c)
@@ -127,15 +145,18 @@
     for step in (-1, 1):
         greet(g_device(step))
         greet(x_device(step))
-
-    z_info = Exchange(NZ, z, z_device, lambda t: msg_info.at[t], in_info, z_send.at[0], z_recv.at[0])
+    for name in loads:
+        if name != "pt":
+            loads[name].start()
+
+    z_info = Exchange(NZ, z, z_device, lambda t: msg.at[t], in_info, z_send.at[0], z_recv.at[0])
     z_cur = Exchange(NZ, z, z_device, lambda t: msg_cur.at[t], in_cur, z_send.at[1], z_recv.at[1])
-    z_tree = Exchange(NZ, z, z_device, lambda t: crow, in_c, z_send.at[2], z_recv.at[2])
-    z_rep = Exchange(NZ, z, z_device, lambda t: rep_c.at[t], rep_d, z_send.at[3], z_recv.at[3])
-    j_info = Exchange(NJ, j, j_device, lambda t: mid_info2, all_info, j_send.at[0], j_recv.at[0])
+    z_rep = Exchange(NZ, z, z_device, lambda t: rep_c.at[t], rep_d, z_send.at[2], z_recv.at[2])
+    z_tree = Exchange(NZ, z, z_device, lambda t: crow, in_c, z_send.at[3], z_recv.at[3])
+    j_info = Exchange(NJ, j, j_device, lambda t: mid_info, all_info, j_send.at[0], j_recv.at[0])
     j_cur = Exchange(NJ, j, j_device, lambda t: mid_cur.at[t], all_cur, j_send.at[1], j_recv.at[1])
-    j_tree = Exchange(NJ, j, j_device, lambda t: mid_c, all_c, j_send.at[2], j_recv.at[2])
-    j_rep = Exchange(NJ, j, j_device, lambda t: rep_a.at[t], rep_b, j_send.at[3], j_recv.at[3])
+    j_rep = Exchange(NJ, j, j_device, lambda t: rep_a.at[t], rep_b, j_send.at[2], j_recv.at[2])
+    j_tree = Exchange(NJ, j, j_device, lambda t: mid_c, all_c, j_send.at[3], j_recv.at[3])
 
     def pair_copy(number, src, dst, device):
         return pltpu.make_async_remote_copy(
@@ -148,13 +169,14 @@
         )
 
     other_core = (x, cell, 1 - c)
-    lin_copy = pair_copy(0, lin, lins.at[c], other_core)
-    tab_copy = pair_copy(1, tab, tabs.at[c], other_core)
+    lin_copy = pair_copy(0, lin_in, lins.at[c], other_core)
+    tab_copy = pair_copy(1, tab_in, tabs.at[c], other_core)
     halo_right = pair_copy(2, win.at[pl.ds(LC, HW)], halo.at[0], g_device(1))
     halo_left = pair_copy(3, win.at[pl.ds(HW, HW)], halo.at[1], g_device(-1))
     x_right = pair_copy(4, up0.at[:, pl.ds(NCELL, 32)], xrows.at[0], x_device(1))
     x_left = pair_copy(5, up0.at[:, pl.ds(32, 32)], xrows.at[1], x_device(-1))
 
+    loaded("pt")
     with jax.named_scope("pairs_out"):
         rows = [pt[f].astype(F32) for f in range(3)]
         rows = jnp.concatenate(rows + [jnp.zeros((CAP, LS), F32)], axis=0)
@@ -169,34 +191,21 @@
         spread = onehot((iota((NZ, LS), 1) >> 3) == iota((NZ, LS), 0))
         info = dot(spread, info.astype(BF16))
         for t in range(NZ):
-            msg_info[t] = info[t : t + 1]
-        own = cur[pl.ds(pl.multiple_of(c * 64, 64), 64), :]
-        lane64 = iota((LS, 64), 1).astype(F32)
-        parts = []
-        for slot in range(CAP):
-            pick = onehot(columns[:, slot : slot + 1] == lane64)
-            parts.append(dot(pick, own).reshape(NZ, NJ, LS))
-        msg_cur[...] = jnp.concatenate(parts, axis=1).astype(BF16)
-
-    pl.semaphore_wait(barrier, (NZ - 1) + (NJ - 1) + 4)
-    z_info.start()
-    lin_copy.start()
-    tab_copy.start()
-    z_cur.start()
-    in_info[pl.ds(z, 1)] = msg_info[pl.ds(z, 1)]
-    in_cur[pl.ds(z, 1)] = msg_cur[pl.ds(z, 1)]
-    lins[pl.ds(c, 1)] = lin[...][None]
-    tabs[pl.ds(c, 1)] = tab[...][None]
-
+            msg[t] = info[t : t + 1]
+    with jax.named_scope("barrier"):
+        pl.semaphore_wait(barrier, (NZ - 1) + (NJ - 1) + 4)
+    with jax.named_scope("start_z_info"):
+        z_info.start()
+    in_info[pl.ds(z, 1)] = msg[pl.ds(z, 1)]
+
+    loaded("cid", "vf", "con")
     with jax.named_scope("weighted"):
         ids = cid[...]
         scale = jnp.zeros((LC, VX), F32)
         for m in range(16):
             scale = jnp.where(ids == m, con[m], scale)
         win[pl.ds(HW, LC), :] = (vf[...].astype(F32) * scale).astype(BF16)
-    halo_right.start()
-    halo_left.start()
-
+    loaded("vrad", "cur", "srad", "host", "lout")
     with jax.named_scope("coarse"):
         weighted = win[pl.ds(HW, LC), :]
         outgoing = dot(weighted, vrad[...])
@@ -207,27 +216,48 @@
         coarse = jnp.sum(leaf.astype(F32) * outgoing, axis=0, keepdims=True)
         coarse = coarse + jnp.sum(leaf_surf * surf_waves, axis=0, keepdims=True)
         crow[...] = coarse
-    z_tree.start()
+    with jax.named_scope("start_z_tree"):
+        z_tree.start()
+        halo_right.start()
+        halo_left.start()
+        lin_copy.start()
+        tab_copy.start()
     in_c[pl.ds(z, 1)] = crow[...][None]
 
+    with jax.named_scope("currents_out"):
+        own = cur[pl.ds(pl.multiple_of(c * 64, 64), 64), :]
+        lane64 = iota((LS, 64), 1).astype(F32)
+        parts = []
+        for slot in range(CAP):
+            pick = onehot(columns[:, slot : slot + 1] == lane64)
+            parts.append(dot(pick, own).reshape(NZ, NJ, LS))
+        msg_cur[...] = jnp.concatenate(parts, axis=1).astype(BF16)
+
+    in_cur[pl.ds(z, 1)] = msg_cur[pl.ds(z, 1)]
+
+    loaded("sv")
     with jax.named_scope("reply_table"):
         own_weighted = win[pl.ds(pl.multiple_of(HW + c * HALF, 16), HALF), :]
         for kind in range(KINDS):
             table[pl.ds(kind * HALF, HALF), :] = dot(own_weighted, sv[kind], 1, 1).astype(BF16)
 
-    z_info.wait_recv()
+    with jax.named_scope("wait_z_info"):
+        z_info.wait_recv()
     for t in range(NZ):
-        mid_info2[pl.ds(t, 1), :] = in_info[t]
-    j_info.start()
-    all_info[pl.ds(j, 1)] = mid_info2[...][None]
-
-    z_tree.wait_recv()
+        mid_info[pl.ds(t, 1), :] = in_info[t]
+    with jax.named_scope("start_j_info"):
+        j_info.start()
+    all_info[pl.ds(j, 1)] = mid_info[...][None]
+    with jax.named_scope("wait_z_tree"):
+        z_tree.wait_recv()
     for t in range(NZ):
         mid_c[pl.ds(t, 1), :] = in_c[t]
     j_tree.start()
+    with jax.named_scope("start_z_cur"):
+        z_cur.start()
     all_c[pl.ds(j, 1)] = mid_c[...][None]
-
-    j_info.wait_recv()
+    with jax.named_scope("wait_j_info"):
+        j_info.wait_recv()
     with jax.named_scope("replies"):
         codes = all_info[...].reshape(LS, LS)
         codes = pltpu.roll(codes, lax.rem(LS - j, LS), 1)
@@ -242,37 +272,10 @@
             rep_a[:, slot] = rep.reshape(NJ, NZ, LS)
     j_rep.start()
     rep_b[pl.ds(j, 1)] = rep_a[pl.ds(j, 1)]
-
-    j_tree.wait_recv()
-    with jax.named_scope("section_rows"):
-        for yy in range(NY):
-            for cc in range(2):
-                up0[cc, pl.ds(32 + yy, NZ, stride=NY), :] = all_c[2 * yy + cc]
-    x_right.start()
-    x_left.start()
-
-    z_cur.wait_recv()
-    with jax.named_scope("regroup_currents"):
-        f_rows[...] = in_cur[...].astype(F32).reshape(NZ * 32, LS)
-        for jj in range(NJ):
-            for slot in range(CAP):
-                block = f_rows[pl.ds(slot * NJ + jj, NZ, stride=32), :]
-                mid_cur[jj, slot] = block.astype(BF16)
-    j_cur.start()
-    all_cur[pl.ds(j, 1)] = mid_cur[pl.ds(j, 1)]
-
-    j_rep.wait_recv()
-    with jax.named_scope("regroup_replies"):
-        f_rows[...] = rep_b[...].astype(F32).reshape(NJ * 64, LS)
-        for zz in range(NZ):
-            blocks = [f_rows[pl.ds(slot * NZ + zz, NJ, stride=64), :] for slot in range(CAP)]
-            rep_c[zz] = jnp.concatenate(blocks, axis=0).astype(BF16)
-    z_rep.start()
-    rep_d[pl.ds(z, 1)] = rep_c[pl.ds(z, 1)]
-
-    halo_right.wait_recv()
-    halo_left.wait_recv()
-    nb_copy.wait()
+    with jax.named_scope("wait_halo"):
+        halo_right.wait_recv()
+        halo_left.wait_recv()
+        loaded("near", "nb")
     with jax.named_scope("near"):
         first = jnp.where(g > 0, 1.0, 0.0)
         last = jnp.where(g < NX * NCELL - 1, 1.0, 0.0)
@@ -291,20 +294,41 @@
         for n in range(NN):
             near = near + dot(gathered[n], nb[n])
 
-    j_cur.wait_recv()
-    with jax.named_scope("coupled_volume"):
-        sums = jnp.zeros((KINDS * HALF, LS), F32)
-        for slot in range(CAP):
-            sums = sums + dot(picks[slot], all_cur[:, slot].reshape(LS, LS), 0, 0)
-        high = sums.astype(BF16)
-        low = (sums - high.astype(F32)).astype(BF16)
-        coupled = jnp.zeros((HALF, VX), F32)
-        for kind in range(KINDS):
-            part = slice(kind * HALF, (kind + 1) * HALF)
-            coupled = coupled + dot(high[part], sv[kind]) + dot(low[part], sv[kind])
-
-    x_right.wait_recv()
-    x_left.wait_recv()
+    with jax.named_scope("wait_j_tree"):
+        j_tree.wait_recv()
+    with jax.named_scope("section_rows"):
+        for yy in range(NY):
+            for cc in range(2):
+                up0[cc, pl.ds(32 + yy, NZ, stride=NY), :] = all_c[2 * yy + cc]
+    x_right.start()
+    x_left.start()
+
+    with jax.named_scope("wait_j_rep"):
+        j_rep.wait_recv()
+    with jax.named_scope("regroup_replies"):
+        f_rows[...] = rep_b[...].astype(F32).reshape(NJ * 64, LS)
+        for zz in range(NZ):
+            blocks = [f_rows[pl.ds(slot * NZ + zz, NJ, stride=64), :] for slot in range(CAP)]
+            rep_c[zz] = jnp.concatenate(blocks, axis=0).astype(BF16)
+    with jax.named_scope("start_z_rep"):
+        z_rep.start()
+    rep_d[pl.ds(z, 1)] = rep_c[pl.ds(z, 1)]
+
+    with jax.named_scope("wait_z_cur"):
+        z_cur.wait_recv()
+    with jax.named_scope("regroup_currents"):
+        f_rows[...] = in_cur[...].astype(F32).reshape(NZ * 32, LS)
+        for jj in range(NJ):
+            for slot in range(CAP):
+                block = f_rows[pl.ds(slot * NJ + jj, NZ, stride=32), :]
+                mid_cur[jj, slot] = block.astype(BF16)
+    j_cur.start()
+    all_cur[pl.ds(j, 1)] = mid_cur[pl.ds(j, 1)]
+
+    with jax.named_scope("wait_x"):
+        x_right.wait_recv()
+        x_left.wait_recv()
+    loaded("tab")
     tab_copy.wait_recv()
     with jax.named_scope("tree"):
         up0[:, pl.ds(0, 32), :] = jnp.where(x > 0, xrows[0], 0.0)
@@ -340,6 +364,7 @@
                 down = terms[level] + jnp.where(is_odd, entry(level, 7), entry(level, 6)) * down
             waves.append(down)
 
+    loaded("lin", "vrec", "srec")
     lin_copy.wait_recv()
     with jax.named_scope("far"):
         far_volume = jnp.zeros((HALF, VX), F32)
@@ -353,10 +378,30 @@
             leaf_here = jnp.where(c == 0, leaf_all[:64], leaf_all[64:])
             incoming = (leaf_here * wave).astype(BF16)
             far_surface = far_surface + dot(incoming, srec[pl.ds(h * KH, KH), :])
+    with jax.named_scope("wait_j_cur"):
+        j_cur.wait_recv()
+    with jax.named_scope("coupled_volume"):
+        sums = jnp.zeros((KINDS * HALF, LS), F32)
+        for slot in range(CAP):
+            sums = sums + dot(picks[slot], all_cur[:, slot].reshape(LS, LS), 0, 0)
+        high = sums.astype(BF16)
+        low = (sums - high.astype(F32)).astype(BF16)
+        coupled = jnp.zeros((HALF, VX), F32)
+        for kind in range(KINDS):
+            part = slice(kind * HALF, (kind + 1) * HALF)
+            coupled = coupled + dot(high[part], sv[kind]) + dot(low[part], sv[kind])
+
+    with jax.named_scope("volume_out"):
         field = vf[pl.ds(pl.multiple_of(c * HALF, 32), HALF), :].astype(F32)
         vout[...] = field + near + far_volume + coupled
 
-    z_rep.wait_recv()
+    with jax.named_scope("wait_sends"):
+        for exchange in (z_info, z_cur, z_tree, j_info, j_cur, j_rep, j_tree):
+            exchange.wait_send()
+        for copy in (lin_copy, tab_copy, halo_right, halo_left, x_right, x_left):
+            copy.wait_send()
+    with jax.named_scope("wait_z_rep"):
+        z_rep.wait_recv()
     with jax.named_scope("coupled_surface"):
         back = rep_d[...].astype(F32)
         sublane64 = iota((64, LS), 0)
@@ -367,10 +412,7 @@
             total = total + dot(pick, mine)
         sout[...] = total
 
-    for exchange in (z_info, z_cur, z_tree, z_rep, j_info, j_cur, j_tree, j_rep):
-        exchange.wait_send()
-    for copy in (lin_copy, tab_copy, halo_right, halo_left, x_right, x_left):
-        copy.wait_send()
+    z_rep.wait_send()
 
 
 def on_device(
@@ -378,26 +420,45 @@
     vol_receive, surf_receive, surface_current, surf_host, leaf_out, leaf_in, level_tables,
     sv_blocks, pair_table,
 ):
+    inputs = (
+        volume_field, contrast_id, contrast, near_index.T, near_blocks, vol_radiation,
+        surf_radiation, vol_receive, surf_receive, surface_current, surf_host.reshape(1, LS),
+        leaf_out, leaf_in, level_tables, sv_blocks, jnp.transpose(pair_table, (2, 1, 0)),
+    )
+    hbm = pl.BlockSpec(memory_space=pltpu.HBM)
     vmem = pl.BlockSpec(memory_space=pltpu.VMEM)
-    specs = [vmem] * 16
-    specs[2] = pl.BlockSpec(memory_space=pltpu.SMEM)
-    specs[4] = pl.BlockSpec(memory_space=pl.ANY)
+    specs = [hbm] * 16
+    shapes = (jax.ShapeDtypeStruct((HALF, VX), F32), jax.ShapeDtypeStruct((64, LS), F32))
     return pl.pallas_call(
         kernel,
-        out_shape=(
-            jax.ShapeDtypeStruct((HALF, VX), F32),
-            jax.ShapeDtypeStruct((64, LS), F32),
-        ),
+        out_shape=shapes,
         in_specs=specs,
         out_specs=(vmem, vmem),
         scratch_shapes=[
+            pltpu.VMEM((LC, VX), BF16),
+            pltpu.VMEM((LC, VX), jnp.int32),
+            pltpu.SMEM((16,), F32),
+            pltpu.VMEM((NN, HALF), jnp.int32),
             pltpu.VMEM((NN, VX, VX), BF16),
+            pltpu.VMEM((VX, KH), BF16),
+            pltpu.VMEM((LS, KH), BF16),
+            pltpu.VMEM((2 * KH, VX), BF16),
+            pltpu.VMEM((2 * KH, LS), BF16),
+            pltpu.VMEM((LS, LS), BF16),
+            pltpu.VMEM((1, LS), jnp.int32),
+            pltpu.VMEM((LC, KH), BF16),
+            pltpu.VMEM((KINDS, LS, VX), BF16),
+            pltpu.VMEM((3, CAP, LS), jnp.int32),
             pltpu.VMEM((WIN, VX), BF16),
             pltpu.VMEM((2, HW, VX), BF16),
             pltpu.VMEM((NZ, 1, LS), F32),
             pltpu.VMEM((NZ, 1, LS), F32),
             pltpu.VMEM((NZ, LS), F32),
             pltpu.VMEM((NJ, NZ, LS), F32),
+            pltpu.VMEM((1, KH), F32),
+            pltpu.VMEM((NZ, 1, KH), F32),
+            pltpu.VMEM((NZ, KH), F32),
+            pltpu.VMEM((NJ, NZ, KH), F32),
             pltpu.VMEM((NZ, 32, LS), BF16),
             pltpu.VMEM((NZ, 32, LS), BF16),
             pltpu.VMEM((512, LS), F32),
@@ -408,10 +469,6 @@
             pltpu.VMEM((NJ, CAP, NZ, LS), BF16),
             pltpu.VMEM((NZ, 32, LS), BF16),
             pltpu.VMEM((NZ, 32, LS), BF16),
-            pltpu.VMEM((1, KH), F32),
-            pltpu.VMEM((NZ, 1, KH), F32),
-            pltpu.VMEM((NZ, KH), F32),
-            pltpu.VMEM((NJ, NZ, KH), F32),
             pltpu.VMEM((2, 128, KH), F32),
             pltpu.VMEM((2, 2, 32, KH), F32),
             pltpu.VMEM((2, 64, KH), F32),
@@ -427,16 +484,12 @@
             pltpu.SemaphoreType.DMA((4, NJ)),
             pltpu.SemaphoreType.DMA((6,)),
             pltpu.SemaphoreType.DMA((6,)),
-            pltpu.SemaphoreType.DMA,
+            pltpu.SemaphoreType.DMA((16,)),
         ],
         compiler_params=pltpu.CompilerParams(
             collective_id=0, has_side_effects=True, vmem_limit_bytes=40 * 1024 * 1024
         ),
-    )(
-        volume_field, contrast_id, contrast, near_index.T, near_blocks, vol_radiation,
-        surf_radiation, vol_receive, surf_receive, surface_current, surf_host.reshape(1, LS),
-        leaf_out, leaf_in, level_tables, sv_blocks, jnp.transpose(pair_table, (2, 1, 0)),
-    )
+    )(*[pltpu.with_memory_space_constraint(array, pltpu.HBM) for array in inputs])
 
 
 def solution(mesh):

time: 64 us -> 43.5 us (0.68)
  the two profiles are of different devices: /device:TPU:1 before, /device:TPU:2 now
where the time goes in v2:
time: 43.5 us; the launch traced here: 43.4 us
  Pallas kernels  41.5 us (95%)
  local copies, waits for them, and re-layouts  1.26 us (3%)
  between operations  0.65 us (1%)
    pallas_call x1, Pallas kernels, on_device(): pl.pallas_call(kernel, out_shape=shapes, in_specs=specs, out_specs=(vmem,...  41.5 us
    unnamed x2, local copies, waits for them, and re-layouts  1.26 us

profile of v2, /device:TPU:2, one launch (start us, length us, event | category | flops | bytes accessed | tf_op | source)
XLA Modules:
  0.0 43.4 jit_solution(11733643572241246922)
XLA Ops:
  0.6 41.5 %shard_map.167 = (f32[96,256]{1,0:T(8,128)S(1)}, f32[64,128]{1,0:T(8,128)S(1)}) custom-call(bf16[192,256]{1,0:T(8,128)(2,1)} %vf_in.1, s32[192,256]{1,0:T(8,128)} %cid_in.1, f32[16]{0:T(128)} %con_in.1, s32[27,96]{1,0:T(8,128)} %bitcast.3, bf16[27,256,256]{2,1,0:T(8,128)(2,1)} %nb_in.1, bf16[256,128]{1,0:T(8,128)(2,1)} %vrad_in.1, bf16[128,128]{1,0:T(8,128)(2,1)} %srad_in.1, ...), custom_call_target="tpu_custom_call" | custom-call | tf_op jit(solution)/shard_map/pallas_call | solution.py:432
  42.1 0.6 %copy.20 = f32[96,256]{1,0:T(8,128)} copy(f32[96,256]{1,0:T(8,128)S(1)} %get-tuple-element.4) | data formatting | bytes 196608
  42.8 0.6 %copy.21 = f32[64,128]{1,0:T(8,128)} copy(f32[64,128]{1,0:T(8,128)S(1)} %get-tuple-element.5) | data formatting | bytes 65536

commit v3 on v2

--- a/solution.py
+++ b/solution.py
@@ -43,40 +43,39 @@
         self.count, self.me, self.device = count, me, device
         self.src, self.dst, self.send, self.recv = src, dst, send, recv
 
-    def copy(self, step, slot):
-        target = lax.rem(self.me + self.offset(step), self.count)
+    def start(self):
+        def body(step, carry):
+            low = lax.div(self.count + 1 - step, 2)
+            offset = jnp.where(lax.rem(step, 2) == 1, low, self.count - low)
+            target = lax.rem(self.me + offset, self.count)
+            pltpu.make_async_remote_copy(
+                src_ref=self.src(target),
+                dst_ref=self.dst.at[self.me],
+                send_sem=self.send,
+                recv_sem=self.recv,
+                device_id=self.device(target),
+                device_id_type=MESH,
+            ).start()
+            return carry
+
+        lax.fori_loop(1, self.count, body, 0)
+
+    def all_blocks(self):
+        blocks = self.dst.at[pl.ds(0, self.count - 1)]
         return pltpu.make_async_remote_copy(
-            src_ref=self.src(target),
-            dst_ref=self.dst.at[slot],
-            send_sem=self.send.at[step],
-            recv_sem=self.recv.at[step],
-            device_id=self.device(target),
+            src_ref=blocks,
+            dst_ref=blocks,
+            send_sem=self.send,
+            recv_sem=self.recv,
+            device_id=self.device(lax.rem(self.me + 1, self.count)),
             device_id_type=MESH,
         )
 
-    def offset(self, step):
-        low = lax.div(self.count + 1 - step, 2)
-        return jnp.where(lax.rem(step, 2) == 1, low, self.count - low)
-
-    def loop(self, body):
-        def wrapped(step, carry):
-            body(step)
-            return carry
-
-        lax.fori_loop(1, self.count, wrapped, 0)
-
-    def start(self):
-        self.loop(lambda step: self.copy(step, self.me).start())
-
     def wait_recv(self):
-        def body(step):
-            source = lax.rem(self.me + self.count - self.offset(step), self.count)
-            self.copy(step, source).wait_recv()
-
-        self.loop(body)
+        self.all_blocks().wait_recv()
 
     def wait_send(self):
-        self.loop(lambda step: self.copy(step, self.me).wait_send())
+        self.all_blocks().wait_send()
 
 
 def kernel(
@@ -478,10 +477,10 @@
             pltpu.VMEM((2, 4, 8, KH), F32),
             pltpu.VMEM((32, 128), F32),
             pltpu.VMEM((NN, HALF, VX), BF16),
-            pltpu.SemaphoreType.DMA((4, NZ)),
-            pltpu.SemaphoreType.DMA((4, NZ)),
-            pltpu.SemaphoreType.DMA((4, NJ)),
-            pltpu.SemaphoreType.DMA((4, NJ)),
+            pltpu.SemaphoreType.DMA((4,)),
+            pltpu.SemaphoreType.DMA((4,)),
+            pltpu.SemaphoreType.DMA((4,)),
+            pltpu.SemaphoreType.DMA((4,)),
             pltpu.SemaphoreType.DMA((6,)),
             pltpu.SemaphoreType.DMA((6,)),
             pltpu.SemaphoreType.DMA((16,)),

time: 43.5 us -> 41.7 us (0.959)
  Pallas kernels: 41.5 us -> 39.7 us
    pallas_call x1, Pallas kernels: 41.5 us -> 39.7 us  [on_device(): pl.pallas_call(kernel, out_shape=shapes, in_specs=specs, out_specs=(vmem,...]
where the time goes in v3:
time: 41.7 us; the launch traced here: 41.6 us
  Pallas kernels  39.7 us (95%)
  local copies, waits for them, and re-layouts  1.26 us (3%)
  between operations  0.65 us (2%)
    pallas_call x1, Pallas kernels, on_device(): pl.pallas_call(kernel, out_shape=shapes, in_specs=specs, out_specs=(vmem,...  39.7 us
    unnamed x2, local copies, waits for them, and re-layouts  1.26 us

profile of v3, /device:TPU:2, one launch (start us, length us, event | category | flops | bytes accessed | tf_op | source)
XLA Modules:
  0.0 41.6 jit_solution(1945072435344252871)
XLA Ops:
  0.6 39.7 %shard_map.167 = (f32[96,256]{1,0:T(8,128)S(1)}, f32[64,128]{1,0:T(8,128)S(1)}) custom-call(bf16[192,256]{1,0:T(8,128)(2,1)} %vf_in.1, s32[192,256]{1,0:T(8,128)} %cid_in.1, f32[16]{0:T(128)} %con_in.1, s32[27,96]{1,0:T(8,128)} %bitcast.3, bf16[27,256,256]{2,1,0:T(8,128)(2,1)} %nb_in.1, bf16[256,128]{1,0:T(8,128)(2,1)} %vrad_in.1, bf16[128,128]{1,0:T(8,128)(2,1)} %srad_in.1, ...), custom_call_target="tpu_custom_call" | custom-call | tf_op jit(solution)/shard_map/pallas_call | solution.py:431
  40.3 0.6 %copy.20 = f32[96,256]{1,0:T(8,128)} copy(f32[96,256]{1,0:T(8,128)S(1)} %get-tuple-element.4) | data formatting | bytes 196608
  41.0 0.6 %copy.21 = f32[64,128]{1,0:T(8,128)} copy(f32[64,128]{1,0:T(8,128)S(1)} %get-tuple-element.5) | data formatting | bytes 65536

commit v4 on v3

--- a/solution.py
+++ b/solution.py
@@ -8,6 +8,8 @@
 MESH = pl.DeviceIdType.MESH
 F32 = jnp.float32
 BF16 = jnp.bfloat16
+
+CUR_AT = 1
 
 NX = 4
 NZ = 16
@@ -60,6 +62,34 @@
 
         lax.fori_loop(1, self.count, body, 0)
 
+    def offset(self, step):
+        low = (self.count + 1 - step) // 2
+        return low if step % 2 == 1 else self.count - low
+
+    def start_each(self, recv):
+        for step in range(1, self.count):
+            target = lax.rem(self.me + self.offset(step), self.count)
+            pltpu.make_async_remote_copy(
+                src_ref=self.src(target),
+                dst_ref=self.dst.at[self.me],
+                send_sem=self.send,
+                recv_sem=recv.at[step],
+                device_id=self.device(target),
+                device_id_type=MESH,
+            ).start()
+
+    def wait_one(self, recv, step):
+        source = lax.rem(self.me + self.count - self.offset(step), self.count)
+        pltpu.make_async_remote_copy(
+            src_ref=self.dst.at[source],
+            dst_ref=self.dst.at[source],
+            send_sem=self.send,
+            recv_sem=recv.at[step],
+            device_id=self.device(source),
+            device_id_type=MESH,
+        ).wait_recv()
+        return source
+
     def all_blocks(self):
         blocks = self.dst.at[pl.ds(0, self.count - 1)]
         return pltpu.make_async_remote_copy(
@@ -84,10 +114,10 @@
     vout, sout,
     vf, cid, con, near_t, nb, vrad, srad, vrec, srec, cur, host, lout, sv, pt, win, halo, msg, in_info, mid_info, all_info, crow, in_c, mid_c, all_c,
     msg_cur, in_cur, f_rows, mid_cur, all_cur,
-    table, rep_a, rep_b, rep_c, rep_d,
+    table, own_rows, near_rows, rep_c, rep_d,
     up0, xrows, up1, up2, up3,
     lins, tabs, idx_pad, gathered,
-    z_send, z_recv, j_send, j_recv, p_send, p_recv, load_sem,
+    z_send, z_recv, j_send, j_recv, p_send, p_recv, own_sem, load_sem,
 ):
     x = lax.axis_index("sec")
     cell = lax.axis_index("cell")
@@ -154,7 +184,7 @@
     z_tree = Exchange(NZ, z, z_device, lambda t: crow, in_c, z_send.at[3], z_recv.at[3])
     j_info = Exchange(NJ, j, j_device, lambda t: mid_info, all_info, j_send.at[0], j_recv.at[0])
     j_cur = Exchange(NJ, j, j_device, lambda t: mid_cur.at[t], all_cur, j_send.at[1], j_recv.at[1])
-    j_rep = Exchange(NJ, j, j_device, lambda t: rep_a.at[t], rep_b, j_send.at[2], j_recv.at[2])
+    j_own = Exchange(NJ, j, j_device, lambda t: own_rows, near_rows, j_send.at[2], j_recv.at[2])
     j_tree = Exchange(NJ, j, j_device, lambda t: mid_c, all_c, j_send.at[3], j_recv.at[3])
 
     def pair_copy(number, src, dst, device):
@@ -191,12 +221,6 @@
         info = dot(spread, info.astype(BF16))
         for t in range(NZ):
             msg[t] = info[t : t + 1]
-    with jax.named_scope("barrier"):
-        pl.semaphore_wait(barrier, (NZ - 1) + (NJ - 1) + 4)
-    with jax.named_scope("start_z_info"):
-        z_info.start()
-    in_info[pl.ds(z, 1)] = msg[pl.ds(z, 1)]
-
     loaded("cid", "vf", "con")
     with jax.named_scope("weighted"):
         ids = cid[...]
@@ -204,6 +228,8 @@
         for m in range(16):
             scale = jnp.where(ids == m, con[m], scale)
         win[pl.ds(HW, LC), :] = (vf[...].astype(F32) * scale).astype(BF16)
+        own_rows[...] = win[pl.ds(pl.multiple_of(HW + c * HALF, 16), HALF), :]
+
     loaded("vrad", "cur", "srad", "host", "lout")
     with jax.named_scope("coarse"):
         weighted = win[pl.ds(HW, LC), :]
@@ -215,6 +241,15 @@
         coarse = jnp.sum(leaf.astype(F32) * outgoing, axis=0, keepdims=True)
         coarse = coarse + jnp.sum(leaf_surf * surf_waves, axis=0, keepdims=True)
         crow[...] = coarse
+    with jax.named_scope("barrier"):
+        pl.semaphore_wait(barrier, (NZ - 1) + (NJ - 1) + 4)
+    with jax.named_scope("start_z_info"):
+        z_info.start()
+    with jax.named_scope("start_j_own"):
+        j_own.start_each(own_sem)
+    in_info[pl.ds(z, 1)] = msg[pl.ds(z, 1)]
+    near_rows[pl.ds(j, 1)] = own_rows[...][None]
+
     with jax.named_scope("start_z_tree"):
         z_tree.start()
         halo_right.start()
@@ -234,12 +269,22 @@
 
     in_cur[pl.ds(z, 1)] = msg_cur[pl.ds(z, 1)]
 
+    if CUR_AT == 1:
+        with jax.named_scope("start_z_cur"):
+            z_cur.start()
+
     loaded("sv")
     with jax.named_scope("reply_table"):
-        own_weighted = win[pl.ds(pl.multiple_of(HW + c * HALF, 16), HALF), :]
-        for kind in range(KINDS):
-            table[pl.ds(kind * HALF, HALF), :] = dot(own_weighted, sv[kind], 1, 1).astype(BF16)
-
+
+        def fill(owner, rows):
+            for kind in range(KINDS):
+                block = dot(rows, sv[kind], 1, 1).astype(BF16)
+                table[pl.ds(owner, 1), pl.ds(kind * HALF, HALF), :] = block[None]
+
+        fill(j, own_rows[...])
+        for step in range(1, NJ):
+            owner = j_own.wait_one(own_sem, step)
+            fill(owner, near_rows[pl.ds(owner, 1)].reshape(HALF, VX))
     with jax.named_scope("wait_z_info"):
         z_info.wait_recv()
     for t in range(NZ):
@@ -247,30 +292,35 @@
     with jax.named_scope("start_j_info"):
         j_info.start()
     all_info[pl.ds(j, 1)] = mid_info[...][None]
+    if CUR_AT == 2:
+        with jax.named_scope("start_z_cur"):
+            z_cur.start()
+    with jax.named_scope("replies"):
+        lane384 = iota((NZ, KINDS * HALF), 1).astype(F32)
+        codes = mid_info[...]
+        codes = codes + HALF * pltpu.roll(codes, LS - 32, 1)
+        for jj in range(NJ):
+            picks = []
+            for slot in range(CAP):
+                at = slot * NJ + jj
+                picks.append(jnp.where(codes[:, at : at + 1] == lane384, 1.0, 0.0))
+            pick = jnp.concatenate(picks, axis=0).astype(BF16)
+            f_rows[pl.ds(jj * 64, 64), :] = dot(pick, table[jj])
+    with jax.named_scope("regroup_replies"):
+        for zz in range(NZ):
+            blocks = [f_rows[pl.ds(slot * NZ + zz, NJ, stride=64), :] for slot in range(CAP)]
+            rep_c[zz] = jnp.concatenate(blocks, axis=0).astype(BF16)
+    with jax.named_scope("start_z_rep"):
+        z_rep.start()
+    rep_d[pl.ds(z, 1)] = rep_c[pl.ds(z, 1)]
+
     with jax.named_scope("wait_z_tree"):
         z_tree.wait_recv()
     for t in range(NZ):
         mid_c[pl.ds(t, 1), :] = in_c[t]
     j_tree.start()
-    with jax.named_scope("start_z_cur"):
-        z_cur.start()
     all_c[pl.ds(j, 1)] = mid_c[...][None]
-    with jax.named_scope("wait_j_info"):
-        j_info.wait_recv()
-    with jax.named_scope("replies"):
-        codes = all_info[...].reshape(LS, LS)
-        codes = pltpu.roll(codes, lax.rem(LS - j, LS), 1)
-        lane384 = iota((LS, KINDS * HALF), 1).astype(F32)
-        picks = []
-        for slot in range(CAP):
-            at = slot * NJ
-            code = codes[:, at : at + 1] + HALF * codes[:, 32 + at : 33 + at]
-            pick = onehot(code == lane384)
-            picks.append(pick)
-            rep = dot(pick, table[...]).astype(BF16)
-            rep_a[:, slot] = rep.reshape(NJ, NZ, LS)
-    j_rep.start()
-    rep_b[pl.ds(j, 1)] = rep_a[pl.ds(j, 1)]
+
     with jax.named_scope("wait_halo"):
         halo_right.wait_recv()
         halo_left.wait_recv()
@@ -302,17 +352,6 @@
     x_right.start()
     x_left.start()
 
-    with jax.named_scope("wait_j_rep"):
-        j_rep.wait_recv()
-    with jax.named_scope("regroup_replies"):
-        f_rows[...] = rep_b[...].astype(F32).reshape(NJ * 64, LS)
-        for zz in range(NZ):
-            blocks = [f_rows[pl.ds(slot * NZ + zz, NJ, stride=64), :] for slot in range(CAP)]
-            rep_c[zz] = jnp.concatenate(blocks, axis=0).astype(BF16)
-    with jax.named_scope("start_z_rep"):
-        z_rep.start()
-    rep_d[pl.ds(z, 1)] = rep_c[pl.ds(z, 1)]
-
     with jax.named_scope("wait_z_cur"):
         z_cur.wait_recv()
     with jax.named_scope("regroup_currents"):
@@ -379,7 +418,16 @@
             far_surface = far_surface + dot(incoming, srec[pl.ds(h * KH, KH), :])
     with jax.named_scope("wait_j_cur"):
         j_cur.wait_recv()
+    with jax.named_scope("wait_j_info"):
+        j_info.wait_recv()
     with jax.named_scope("coupled_volume"):
+        codes = pltpu.roll(all_info[...].reshape(LS, LS), lax.rem(LS - j, LS), 1)
+        lane384 = iota((LS, KINDS * HALF), 1).astype(F32)
+        picks = []
+        for slot in range(CAP):
+            at = slot * NJ
+            code = codes[:, at : at + 1] + HALF * codes[:, 32 + at : 33 + at]
+            picks.append(onehot(code == lane384))
         sums = jnp.zeros((KINDS * HALF, LS), F32)
         for slot in range(CAP):
             sums = sums + dot(picks[slot], all_cur[:, slot].reshape(LS, LS), 0, 0)
@@ -395,7 +443,7 @@
         vout[...] = field + near + far_volume + coupled
 
     with jax.named_scope("wait_sends"):
-        for exchange in (z_info, z_cur, z_tree, j_info, j_cur, j_rep, j_tree):
+        for exchange in (z_info, z_cur, z_tree, j_info, j_cur, j_own, j_tree):
             exchange.wait_send()
         for copy in (lin_copy, tab_copy, halo_right, halo_left, x_right, x_left):
             copy.wait_send()
@@ -463,9 +511,9 @@
             pltpu.VMEM((512, LS), F32),
             pltpu.VMEM((NJ, CAP, NZ, LS), BF16),
             pltpu.VMEM((NJ, CAP, NZ, LS), BF16),
-            pltpu.VMEM((KINDS * HALF, LS), BF16),
-            pltpu.VMEM((NJ, CAP, NZ, LS), BF16),
-            pltpu.VMEM((NJ, CAP, NZ, LS), BF16),
+            pltpu.VMEM((NJ, KINDS * HALF, LS), BF16),
+            pltpu.VMEM((HALF, VX), BF16),
+            pltpu.VMEM((NJ, HALF, VX), BF16),
             pltpu.VMEM((NZ, 32, LS), BF16),
             pltpu.VMEM((NZ, 32, LS), BF16),
             pltpu.VMEM((2, 128, KH), F32),
@@ -483,6 +531,7 @@
             pltpu.SemaphoreType.DMA((4,)),
             pltpu.SemaphoreType.DMA((6,)),
             pltpu.SemaphoreType.DMA((6,)),
+            pltpu.SemaphoreType.DMA((NJ,)),
             pltpu.SemaphoreType.DMA((16,)),
         ],
         compiler_params=pltpu.CompilerParams(

time: 41.7 us -> 36.4 us (0.87)
  the two profiles are of different devices: /device:TPU:2 before, /device:TPU:1 now
where the time goes in v4:
time: 36.4 us; the launch traced here: 36.3 us
  Pallas kernels  34.4 us (95%)
  local copies, waits for them, and re-layouts  1.26 us (3%)
  between operations  0.65 us (2%)
    pallas_call x1, Pallas kernels, on_device(): pl.pallas_call(kernel, out_shape=shapes, in_specs=specs, out_specs=(vmem,...  34.4 us
    unnamed x2, local copies, waits for them, and re-layouts  1.26 us

profile of v4, /device:TPU:1, one launch (start us, length us, event | category | flops | bytes accessed | tf_op | source)
XLA Modules:
  0.0 36.3 jit_solution(10996164619110408662)
XLA Ops:
  0.6 34.4 %shard_map.167 = (f32[96,256]{1,0:T(8,128)S(1)}, f32[64,128]{1,0:T(8,128)S(1)}) custom-call(bf16[192,256]{1,0:T(8,128)(2,1)} %vf_in.1, s32[192,256]{1,0:T(8,128)} %cid_in.1, f32[16]{0:T(128)} %con_in.1, s32[27,96]{1,0:T(8,128)} %bitcast.3, bf16[27,256,256]{2,1,0:T(8,128)(2,1)} %nb_in.1, bf16[256,128]{1,0:T(8,128)(2,1)} %vrad_in.1, bf16[128,128]{1,0:T(8,128)(2,1)} %srad_in.1, ...), custom_call_target="tpu_custom_call" | custom-call | tf_op jit(solution)/shard_map/pallas_call | solution.py:479
  35.0 0.6 %copy.20 = f32[96,256]{1,0:T(8,128)} copy(f32[96,256]{1,0:T(8,128)S(1)} %get-tuple-element.4) | data formatting | bytes 196608
  35.7 0.6 %copy.21 = f32[64,128]{1,0:T(8,128)} copy(f32[64,128]{1,0:T(8,128)S(1)} %get-tuple-element.5) | data formatting | bytes 65536

commit v5 on v4

--- a/solution.py
+++ b/solution.py
@@ -8,8 +8,6 @@
 MESH = pl.DeviceIdType.MESH
 F32 = jnp.float32
 BF16 = jnp.bfloat16
-
-CUR_AT = 1
 
 NX = 4
 NZ = 16
@@ -243,10 +241,10 @@
         crow[...] = coarse
     with jax.named_scope("barrier"):
         pl.semaphore_wait(barrier, (NZ - 1) + (NJ - 1) + 4)
+    with jax.named_scope("start_j_own"):
+        j_own.start_each(own_sem)
     with jax.named_scope("start_z_info"):
         z_info.start()
-    with jax.named_scope("start_j_own"):
-        j_own.start_each(own_sem)
     in_info[pl.ds(z, 1)] = msg[pl.ds(z, 1)]
     near_rows[pl.ds(j, 1)] = own_rows[...][None]
 
@@ -269,9 +267,8 @@
 
     in_cur[pl.ds(z, 1)] = msg_cur[pl.ds(z, 1)]
 
-    if CUR_AT == 1:
-        with jax.named_scope("start_z_cur"):
-            z_cur.start()
+    with jax.named_scope("start_z_cur"):
+        z_cur.start()
 
     loaded("sv")
     with jax.named_scope("reply_table"):
@@ -292,9 +289,12 @@
     with jax.named_scope("start_j_info"):
         j_info.start()
     all_info[pl.ds(j, 1)] = mid_info[...][None]
-    if CUR_AT == 2:
-        with jax.named_scope("start_z_cur"):
-            z_cur.start()
+    with jax.named_scope("wait_z_tree"):
+        z_tree.wait_recv()
+    for t in range(NZ):
+        mid_c[pl.ds(t, 1), :] = in_c[t]
+    j_tree.start()
+    all_c[pl.ds(j, 1)] = mid_c[...][None]
     with jax.named_scope("replies"):
         lane384 = iota((NZ, KINDS * HALF), 1).astype(F32)
         codes = mid_info[...]
@@ -314,12 +314,16 @@
         z_rep.start()
     rep_d[pl.ds(z, 1)] = rep_c[pl.ds(z, 1)]
 
-    with jax.named_scope("wait_z_tree"):
-        z_tree.wait_recv()
-    for t in range(NZ):
-        mid_c[pl.ds(t, 1), :] = in_c[t]
-    j_tree.start()
-    all_c[pl.ds(j, 1)] = mid_c[...][None]
+    with jax.named_scope("wait_z_cur"):
+        z_cur.wait_recv()
+    with jax.named_scope("regroup_currents"):
+        f_rows[...] = in_cur[...].astype(F32).reshape(NZ * 32, LS)
+        for jj in range(NJ):
+            for slot in range(CAP):
+                block = f_rows[pl.ds(slot * NJ + jj, NZ, stride=32), :]
+                mid_cur[jj, slot] = block.astype(BF16)
+    j_cur.start()
+    all_cur[pl.ds(j, 1)] = mid_cur[pl.ds(j, 1)]
 
     with jax.named_scope("wait_halo"):
         halo_right.wait_recv()
@@ -339,9 +343,6 @@
         for n in range(NN):
             pick = onehot(slots[:, n : n + 1] == lane_w)
             gathered[n] = dot(pick, window).astype(BF16)
-        near = jnp.zeros((HALF, VX), F32)
-        for n in range(NN):
-            near = near + dot(gathered[n], nb[n])
 
     with jax.named_scope("wait_j_tree"):
         j_tree.wait_recv()
@@ -352,70 +353,11 @@
     x_right.start()
     x_left.start()
 
-    with jax.named_scope("wait_z_cur"):
-        z_cur.wait_recv()
-    with jax.named_scope("regroup_currents"):
-        f_rows[...] = in_cur[...].astype(F32).reshape(NZ * 32, LS)
-        for jj in range(NJ):
-            for slot in range(CAP):
-                block = f_rows[pl.ds(slot * NJ + jj, NZ, stride=32), :]
-                mid_cur[jj, slot] = block.astype(BF16)
-    j_cur.start()
-    all_cur[pl.ds(j, 1)] = mid_cur[pl.ds(j, 1)]
-
-    with jax.named_scope("wait_x"):
-        x_right.wait_recv()
-        x_left.wait_recv()
-    loaded("tab")
-    tab_copy.wait_recv()
-    with jax.named_scope("tree"):
-        up0[:, pl.ds(0, 32), :] = jnp.where(x > 0, xrows[0], 0.0)
-        up0[:, pl.ds(96, 32), :] = jnp.where(x < NX - 1, xrows[1], 0.0)
-        ups = [up0, up1, up2, up3]
-        waves = []
-        for h in range(2):
-
-            def entry(level, number):
-                return tabs[h, level, pl.ds(number, 1), :]
-
-            for level in range(3):
-                count = 64 >> level
-                even = ups[level][h, pl.ds(0, count, stride=2), :]
-                odd = ups[level][h, pl.ds(1, count, stride=2), :]
-                ups[level + 1][h] = entry(level, 4) * even + entry(level, 5) * odd
-            terms = []
-            for level in range(4):
-                at = (32 + cell) >> level
-                is_odd = (at & 1) == 1
-
-                def row(offset):
-                    return ups[level][h, pl.ds(at + offset, 1), :]
-
-                term = jnp.where(is_odd, entry(level, 0) * row(-3), 0.0)
-                term = term + entry(level, 1) * row(-2)
-                term = term + entry(level, 2) * row(2)
-                term = term + jnp.where(is_odd, 0.0, entry(level, 3) * row(3))
-                terms.append(term)
-            down = terms[3]
-            for level in (2, 1, 0):
-                is_odd = (((32 + cell) >> level) & 1) == 1
-                down = terms[level] + jnp.where(is_odd, entry(level, 7), entry(level, 6)) * down
-            waves.append(down)
-
-    loaded("lin", "vrec", "srec")
-    lin_copy.wait_recv()
-    with jax.named_scope("far"):
-        far_volume = jnp.zeros((HALF, VX), F32)
-        far_surface = jnp.zeros((64, LS), F32)
-        for h in range(2):
-            wave = waves[h]
-            leaf_own = lins[h, pl.ds(pl.multiple_of(c * HALF, 32), HALF), :].astype(F32)
-            incoming = (leaf_own * wave).astype(BF16)
-            far_volume = far_volume + dot(incoming, vrec[pl.ds(h * KH, KH), :])
-            leaf_all = dot(host_t, lins[h], 0, 0)
-            leaf_here = jnp.where(c == 0, leaf_all[:64], leaf_all[64:])
-            incoming = (leaf_here * wave).astype(BF16)
-            far_surface = far_surface + dot(incoming, srec[pl.ds(h * KH, KH), :])
+    with jax.named_scope("near_blocks"):
+        near = jnp.zeros((HALF, VX), F32)
+        for n in range(NN):
+            near = near + dot(gathered[n], nb[n])
+
     with jax.named_scope("wait_j_cur"):
         j_cur.wait_recv()
     with jax.named_scope("wait_j_info"):
@@ -438,6 +380,59 @@
             part = slice(kind * HALF, (kind + 1) * HALF)
             coupled = coupled + dot(high[part], sv[kind]) + dot(low[part], sv[kind])
 
+    with jax.named_scope("wait_x"):
+        x_right.wait_recv()
+        x_left.wait_recv()
+    loaded("tab")
+    tab_copy.wait_recv()
+    with jax.named_scope("tree"):
+        up0[:, pl.ds(0, 32), :] = jnp.where(x > 0, xrows[0], 0.0)
+        up0[:, pl.ds(96, 32), :] = jnp.where(x < NX - 1, xrows[1], 0.0)
+        ups = [up0, up1, up2, up3]
+        waves = []
+        for h in range(2):
+
+            def entry(level, number):
+                return tabs[h, level, pl.ds(number, 1), :]
+
+            for level in range(3):
+                count = 64 >> level
+                even = ups[level][h, pl.ds(0, count, stride=2), :]
+                odd = ups[level][h, pl.ds(1, count, stride=2), :]
+                ups[level + 1][h] = entry(level, 4) * even + entry(level, 5) * odd
+            terms = []
+            for level in range(4):
+                at = (32 + cell) >> level
+                is_odd = (at & 1) == 1
+
+                def row(offset):
+                    return ups[level][h, pl.ds(at + offset, 1), :]
+
+                term = jnp.where(is_odd, entry(level, 0) * row(-3), 0.0)
+                term = term + entry(level, 1) * row(-2)
+                term = term + entry(level, 2) * row(2)
+                term = term + jnp.where(is_odd, 0.0, entry(level, 3) * row(3))
+                terms.append(term)
+            down = terms[3]
+            for level in (2, 1, 0):
+                is_odd = (((32 + cell) >> level) & 1) == 1
+                down = terms[level] + jnp.where(is_odd, entry(level, 7), entry(level, 6)) * down
+            waves.append(down)
+
+    loaded("lin", "vrec", "srec")
+    lin_copy.wait_recv()
+    with jax.named_scope("far"):
+        far_volume = jnp.zeros((HALF, VX), F32)
+        far_surface = jnp.zeros((64, LS), F32)
+        for h in range(2):
+            wave = waves[h]
+            leaf_own = lins[h, pl.ds(pl.multiple_of(c * HALF, 32), HALF), :].astype(F32)
+            incoming = (leaf_own * wave).astype(BF16)
+            far_volume = far_volume + dot(incoming, vrec[pl.ds(h * KH, KH), :])
+            leaf_all = dot(host_t, lins[h], 0, 0)
+            leaf_here = jnp.where(c == 0, leaf_all[:64], leaf_all[64:])
+            incoming = (leaf_here * wave).astype(BF16)
+            far_surface = far_surface + dot(incoming, srec[pl.ds(h * KH, KH), :])
     with jax.named_scope("volume_out"):
         field = vf[pl.ds(pl.multiple_of(c * HALF, 32), HALF), :].astype(F32)
         vout[...] = field + near + far_volume + coupled

time: 36.4 us -> 34.9 us (0.959)
  Pallas kernels: 34.4 us -> 32.8 us
    pallas_call x1, Pallas kernels: 34.4 us -> 32.8 us  [on_device(): pl.pallas_call(kernel, out_shape=shapes, in_specs=specs, out_specs=(vmem,...]
where the time goes in v5:
time: 34.9 us; the launch traced here: 34.7 us
  Pallas kernels  32.8 us (94%)
  local copies, waits for them, and re-layouts  1.26 us (4%)
  between operations  0.65 us (2%)
    pallas_call x1, Pallas kernels, on_device(): pl.pallas_call(kernel, out_shape=shapes, in_specs=specs, out_specs=(vmem,...  32.8 us
    unnamed x2, local copies, waits for them, and re-layouts  1.26 us

profile of v5, /device:TPU:1, one launch (start us, length us, event | category | flops | bytes accessed | tf_op | source)
XLA Modules:
  0.0 34.7 jit_solution(16055026068155988645)
XLA Ops:
  0.6 32.8 %shard_map.167 = (f32[96,256]{1,0:T(8,128)S(1)}, f32[64,128]{1,0:T(8,128)S(1)}) custom-call(bf16[192,256]{1,0:T(8,128)(2,1)} %vf_in.1, s32[192,256]{1,0:T(8,128)} %cid_in.1, f32[16]{0:T(128)} %con_in.1, s32[27,96]{1,0:T(8,128)} %bitcast.3, bf16[27,256,256]{2,1,0:T(8,128)(2,1)} %nb_in.1, bf16[256,128]{1,0:T(8,128)(2,1)} %vrad_in.1, bf16[128,128]{1,0:T(8,128)(2,1)} %srad_in.1, ...), custom_call_target="tpu_custom_call" | custom-call | tf_op jit(solution)/shard_map/pallas_call | solution.py:474
  33.5 0.6 %copy.20 = f32[96,256]{1,0:T(8,128)} copy(f32[96,256]{1,0:T(8,128)S(1)} %get-tuple-element.4) | data formatting | bytes 196608
  34.1 0.6 %copy.21 = f32[64,128]{1,0:T(8,128)} copy(f32[64,128]{1,0:T(8,128)S(1)} %get-tuple-element.5) | data formatting | bytes 65536

commit v6 on v5

--- a/solution.py
+++ b/solution.py
@@ -239,6 +239,17 @@
         coarse = jnp.sum(leaf.astype(F32) * outgoing, axis=0, keepdims=True)
         coarse = coarse + jnp.sum(leaf_surf * surf_waves, axis=0, keepdims=True)
         crow[...] = coarse
+    with jax.named_scope("currents_out"):
+        own = cur[pl.ds(pl.multiple_of(c * 64, 64), 64), :]
+        lane64 = iota((LS, 64), 1).astype(F32)
+        parts = []
+        for slot in range(CAP):
+            pick = onehot(columns[:, slot : slot + 1] == lane64)
+            parts.append(dot(pick, own).reshape(NZ, NJ, LS))
+        msg_cur[...] = jnp.concatenate(parts, axis=1).astype(BF16)
+
+    in_cur[pl.ds(z, 1)] = msg_cur[pl.ds(z, 1)]
+
     with jax.named_scope("barrier"):
         pl.semaphore_wait(barrier, (NZ - 1) + (NJ - 1) + 4)
     with jax.named_scope("start_j_own"):
@@ -255,17 +266,6 @@
         lin_copy.start()
         tab_copy.start()
     in_c[pl.ds(z, 1)] = crow[...][None]
-
-    with jax.named_scope("currents_out"):
-        own = cur[pl.ds(pl.multiple_of(c * 64, 64), 64), :]
-        lane64 = iota((LS, 64), 1).astype(F32)
-        parts = []
-        for slot in range(CAP):
-            pick = onehot(columns[:, slot : slot + 1] == lane64)
-            parts.append(dot(pick, own).reshape(NZ, NJ, LS))
-        msg_cur[...] = jnp.concatenate(parts, axis=1).astype(BF16)
-
-    in_cur[pl.ds(z, 1)] = msg_cur[pl.ds(z, 1)]
 
     with jax.named_scope("start_z_cur"):
         z_cur.start()

time: 34.9 us -> 34.8 us (level)
  no operation moved by 1% of the time
where the time goes in v6:
time: 34.8 us; the launch traced here: 34.7 us
  Pallas kernels  32.8 us (94%)
  local copies, waits for them, and re-layouts  1.26 us (4%)
  between operations  0.65 us (2%)
    pallas_call x1, Pallas kernels, on_device(): pl.pallas_call(kernel, out_shape=shapes, in_specs=specs, out_specs=(vmem,...  32.8 us
    unnamed x2, local copies, waits for them, and re-layouts  1.26 us

profile of v6, /device:TPU:1, one launch (start us, length us, event | category | flops | bytes accessed | tf_op | source)
XLA Modules:
  0.0 34.7 jit_solution(7479579071895999991)
XLA Ops:
  0.6 32.8 %shard_map.167 = (f32[96,256]{1,0:T(8,128)S(1)}, f32[64,128]{1,0:T(8,128)S(1)}) custom-call(bf16[192,256]{1,0:T(8,128)(2,1)} %vf_in.1, s32[192,256]{1,0:T(8,128)} %cid_in.1, f32[16]{0:T(128)} %con_in.1, s32[27,96]{1,0:T(8,128)} %bitcast.3, bf16[27,256,256]{2,1,0:T(8,128)(2,1)} %nb_in.1, bf16[256,128]{1,0:T(8,128)(2,1)} %vrad_in.1, bf16[128,128]{1,0:T(8,128)(2,1)} %srad_in.1, ...), custom_call_target="tpu_custom_call" | custom-call | tf_op jit(solution)/shard_map/pallas_call | solution.py:474
  33.4 0.6 %copy.20 = f32[96,256]{1,0:T(8,128)} copy(f32[96,256]{1,0:T(8,128)S(1)} %get-tuple-element.4) | data formatting | bytes 196608
  34.0 0.6 %copy.21 = f32[64,128]{1,0:T(8,128)} copy(f32[64,128]{1,0:T(8,128)S(1)} %get-tuple-element.5) | data formatting | bytes 65536

commit v7 on v6

--- a/solution.py
+++ b/solution.py
@@ -261,14 +261,14 @@
 
     with jax.named_scope("start_z_tree"):
         z_tree.start()
+    in_c[pl.ds(z, 1)] = crow[...][None]
+
+    with jax.named_scope("start_z_cur"):
+        z_cur.start()
         halo_right.start()
         halo_left.start()
         lin_copy.start()
         tab_copy.start()
-    in_c[pl.ds(z, 1)] = crow[...][None]
-
-    with jax.named_scope("start_z_cur"):
-        z_cur.start()
 
     loaded("sv")
     with jax.named_scope("reply_table"):

time: 34.8 us -> 34.8 us (level)
  no operation moved by 1% of the time
where the time goes in v7:
time: 34.8 us; the launch traced here: 34.7 us
  Pallas kernels  32.8 us (94%)
  local copies, waits for them, and re-layouts  1.26 us (4%)
  between operations  0.65 us (2%)
    pallas_call x1, Pallas kernels, on_device(): pl.pallas_call(kernel, out_shape=shapes, in_specs=specs, out_specs=(vmem,...  32.8 us
    unnamed x2, local copies, waits for them, and re-layouts  1.26 us

profile of v7, /device:TPU:1, one launch (start us, length us, event | category | flops | bytes accessed | tf_op | source)
XLA Modules:
  0.0 34.7 jit_solution(11738378358578546488)
XLA Ops:
  0.6 32.8 %shard_map.167 = (f32[96,256]{1,0:T(8,128)S(1)}, f32[64,128]{1,0:T(8,128)S(1)}) custom-call(bf16[192,256]{1,0:T(8,128)(2,1)} %vf_in.1, s32[192,256]{1,0:T(8,128)} %cid_in.1, f32[16]{0:T(128)} %con_in.1, s32[27,96]{1,0:T(8,128)} %bitcast.3, bf16[27,256,256]{2,1,0:T(8,128)(2,1)} %nb_in.1, bf16[256,128]{1,0:T(8,128)(2,1)} %vrad_in.1, bf16[128,128]{1,0:T(8,128)(2,1)} %srad_in.1, ...), custom_call_target="tpu_custom_call" | custom-call | tf_op jit(solution)/shard_map/pallas_call | solution.py:474
  33.4 0.6 %copy.20 = f32[96,256]{1,0:T(8,128)} copy(f32[96,256]{1,0:T(8,128)S(1)} %get-tuple-element.4) | data formatting | bytes 196608
  34.0 0.6 %copy.21 = f32[64,128]{1,0:T(8,128)} copy(f32[64,128]{1,0:T(8,128)S(1)} %get-tuple-element.5) | data formatting | bytes 65536
